TPU v7x, 32 devices: a whole 2x2x4 slice. The times are simulated.
32 devices in a mesh: src: 8 (over z, y), dst: 4 (over x, core).
Axes of the slice: x: 2, y: 2, z: 4, core: 2. Of those that a mesh axis runs over, the one named last changes fastest.
Arguments:
- features: bfloat16 [4096, 128], P(('src', 'dst')), may hold values from -6 to 6
- weight: bfloat16 [128, 256], replicated, may hold values from -0.5 to 0.5
- bias: float32 [256], replicated, may hold values from -3 to 3
- tile_index: int32 [8, 4, 8], P('src', 'dst'), may hold values from 0 to 31, as said below
- edge_count: int32 [8, 4, 8], P('src', 'dst'), may hold values from 0 to 64, as said below
- edge_pos: int32 [8, 4, 8, 64], P('src', 'dst'), may hold values from 0 to 16383
- edge_weight: bfloat16 [8, 4, 8, 64], P('src', 'dst'), may hold values from 0.099609375 to 0.3984375
- grad_out: bfloat16 [4096, 256], P(('src', 'dst')), may hold values from -15 to 15
Outputs:
- hidden: bfloat16 [4096, 256], P(('src', 'dst'))
- input_grad: bfloat16 [4096, 128], P(('src', 'dst'))
- weight_grad: float32 [128, 256], replicated
- bias_grad: float32 [256], replicated
Inputs may be any that keep to these rules, and one draw needn't show every extreme that they name: `tile_index`: the 8 entries of one device are distinct; id c names tile row c // 4 and tile column c % 4 of the device's block of 1024 target rows and 512 source columns. `edge_count`: on each device the live slots (count 1 or more) come first and all later slots have count 0; slot 0 is always live; some device has all 8 slots live; every device has a slot with 64 edges. `edge_pos`: row * 128 + column inside the tile; positions may repeat within a tile.
All inputs are finite; a program needn't handle non-finite values.
Results may differ from a plain program's by a relative error of at most 0.0065.
Values may be sent and summed in bfloat16 or wider, within the bound.
A program may use at most 64 MiB of HBM per device.

v0:
```python
import math

import jax
import jax.numpy as jnp
from jax import lax
from jax.sharding import PartitionSpec as P

F_IN = 128
TILE = 128


def build_tiles(positions, weights, counts):
    slot_ids = lax.broadcasted_iota(jnp.int32, positions.shape, 1)
    live_mask = slot_ids < counts[:, None]
    lane_ids = lax.broadcasted_iota(jnp.int32, (1, 1, TILE), 2)
    row_hot = jnp.where(
        ((positions // TILE)[:, :, None] == lane_ids) & live_mask[:, :, None],
        weights[:, :, None],
        jnp.zeros((), jnp.bfloat16),
    )
    col_hot = jnp.where(
        (positions % TILE)[:, :, None] == lane_ids,
        jnp.ones((), jnp.bfloat16),
        jnp.zeros((), jnp.bfloat16),
    )
    summed = jnp.einsum("bei,bej->bij", row_hot, col_hot, preferred_element_type=jnp.float32)
    return summed.astype(jnp.bfloat16)


def body(features, weight, bias, tile_index, edge_count, edge_pos, edge_weight, grad_out):
    own_rows = features.shape[0]
    tile_ids = tile_index.reshape(-1)
    counts = edge_count.reshape(-1)
    slot_total = counts.shape[0]
    positions = edge_pos.reshape(slot_total, -1)
    weights = edge_weight.reshape(slot_total, -1)
    tile_block = math.gcd(slot_total, 16)
    source_rows = lax.all_gather(features, "dst", axis=0, tiled=True)
    source_tiles = source_rows.reshape(-1, TILE, F_IN)
    src_tile_total = source_tiles.shape[0]
    target_rows = own_rows * lax.axis_size("src")
    target_tile_total = target_rows // TILE
    loop_turns = slot_total // tile_block

    def block_tiles(block_index):
        block_start = block_index * tile_block
        tile_slots = lax.dynamic_slice_in_dim(tile_ids, block_start, tile_block)
        dense_tiles = build_tiles(
            lax.dynamic_slice_in_dim(positions, block_start, tile_block),
            lax.dynamic_slice_in_dim(weights, block_start, tile_block),
            lax.dynamic_slice_in_dim(counts, block_start, tile_block),
        )
        return (tile_slots // src_tile_total, tile_slots % src_tile_total, dense_tiles)

    def forward_block(block_index, running):
        target_ids, source_ids, dense_tiles = block_tiles(block_index)
        inputs = jnp.take(source_tiles, source_ids, axis=0)
        contrib = jnp.einsum(
            "bij,bjf->bif", dense_tiles, inputs, preferred_element_type=jnp.float32
        )
        return running.at[target_ids].add(contrib)

    partial_sums = lax.fori_loop(
        0, loop_turns, forward_block, jnp.zeros((target_tile_total, TILE, F_IN), jnp.float32)
    )
    aggregated = lax.psum_scatter(
        partial_sums.reshape(target_rows, F_IN), "src", scatter_dimension=0, tiled=True
    ).astype(jnp.bfloat16)
    preact = jnp.dot(aggregated, weight, preferred_element_type=jnp.float32) + bias
    hidden = jax.nn.silu(preact).astype(jnp.bfloat16)
    sigmoid_pre = jax.nn.sigmoid(preact)
    grad_pre = (
        grad_out.astype(jnp.float32) * sigmoid_pre * (1.0 + preact * (1.0 - sigmoid_pre))
    ).astype(jnp.bfloat16)
    node_total = own_rows * lax.axis_size("src") * lax.axis_size("dst")
    node_scale = 1.0 / math.sqrt(node_total)
    weight_sum, bias_sum = lax.psum(
        (
            jnp.einsum("nf,nh->fh", aggregated, grad_pre, preferred_element_type=jnp.float32),
            jnp.sum(grad_pre.astype(jnp.float32), axis=0),
        ),
        ("src", "dst"),
    )
    target_grad = lax.all_gather(grad_pre, "src", axis=0, tiled=True)
    target_back = jnp.einsum(
        "nh,fh->nf", target_grad, weight, preferred_element_type=jnp.float32
    ).astype(jnp.bfloat16)
    back_tiles = target_back.reshape(target_tile_total, TILE, F_IN)

    def backward_block(block_index, running):
        target_ids, source_ids, dense_tiles = block_tiles(block_index)
        grad_tiles = jnp.take(back_tiles, target_ids, axis=0)
        contrib = jnp.einsum(
            "bij,bif->bjf", dense_tiles, grad_tiles, preferred_element_type=jnp.float32
        )
        return running.at[source_ids].add(contrib)

    back_sums = lax.fori_loop(
        0, loop_turns, backward_block, jnp.zeros((src_tile_total, TILE, F_IN), jnp.float32)
    )
    input_grad = lax.psum_scatter(
        back_sums.reshape(-1, F_IN), "dst", scatter_dimension=0, tiled=True
    ).astype(jnp.bfloat16)
    return (hidden, input_grad, weight_sum * node_scale, bias_sum * node_scale)


def solution(mesh):
    placed = (
        P(("src", "dst"), None),
        P(),
        P(),
        P("src", "dst", None),
        P("src", "dst", None),
        P("src", "dst", None, None),
        P("src", "dst", None, None),
        P(("src", "dst"), None),
    )
    return jax.shard_map(
        body,
        mesh=mesh,
        in_specs=placed,
        out_specs=(P(("src", "dst"), None), P(("src", "dst"), None), P(), P()),
        check_vma=False,
    )
```

profile of v0, /device:TPU:0, one launch (start us, length us, event | category | flops | bytes accessed | tf_op | source)
XLA Modules:
  0.0 269.5 jit_solution(892359262288990105)
XLA Ops:
  7.2 0.0 reduce-scatter.3.cloned.1.call-start
  7.2 0.7 fusion.26
  7.9 0.7 add_select_fusion.1
  8.6 0.7 copy-done.8
  9.3 0.1 iota_compare_fusion.2
  9.4 6.7 %all_gather.6 = bf16[512,128]{1,0:T(8,128)(2,1)S(1)} all-gather(bf16[128,128]{1,0:T(8,128)(2,1)} %param.8), channel_id=1, replica_groups=mesh['src'=8,'dst'=4] {'dst'}, dimensions={0}, use_global_device_ids=true | all-gather | bytes 163840 | tf_op jit(solution)/shard_map/all_gather | solution.py:38
  16.1 0.6 gather_fusion
  16.7 0.7 copy-done.5
  17.3 0.7 convolution_convert_fusion.1
  18.0 0.3 fusion.2
  18.4 1.0 scatter_fusion
  19.4 0.8 copy-done.1
  20.2 0.0 reduce-scatter.3.cloned.1.call-update
  20.2 0.0 all-reduce.2.cloned.1.call-start
  20.3 63.7 %reduce-scatter.3.cloned.1.call-done = f32[128,128]{1,0:T(8,128)} async-done(((f32[1024,128]{1,0:T(8,128)}), f32[128,128]{1,0:T(8,128)}) %reduce-scatter.3.cloned.1.call-update) | async-done | bytes 65552 | tf_op jit(solution)/shard_map/reduce_scatter | solution.py:66
  84.0 1.7 convert_reduce_fusion
  85.6 31.6 %all_gather.7 = bf16[1024,256]{1,0:T(8,128)(2,1)S(1)} all-gather(bf16[128,256]{1,0:T(8,128)(2,1)S(1)} %get-tuple-element.37), channel_id=1, replica_groups=mesh['src'=8,'dst'=4] {'src'}, dimensions={0}, use_global_device_ids=true | all-gather | bytes 589824 | tf_op jit(solution)/shard_map/all_gather | solution.py:84
  117.2 0.9 fusion.19
  118.1 0.0 all-reduce.2.cloned.1.call-update
  118.1 0.0 reduce-scatter.5.cloned.1.call-start
  118.1 0.3 convolution_convert_fusion
  118.4 0.6 gather_fusion.1
  119.0 0.3 fusion
  119.4 1.0 scatter_fusion.1
  120.4 0.7 copy-done.2
  121.1 0.0 reduce-scatter.5.cloned.1.call-update
  121.1 37.8 %psum.15 = f32[256]{0:T(256)S(1)} all-reduce(f32[256]{0:T(256)S(1)} %get-tuple-element.36), channel_id=1, replica_groups=mesh['src'=8,'dst'=4] {'src','dst'}, use_global_device_ids=true, to_apply=%region_6.7 | all-reduce | flops 256 | bytes 2048 | tf_op jit(solution)/shard_map/psum | solution.py:77
  158.9 0.6 broadcast_multiply_fusion.1
  159.5 80.3 %all-reduce.2.cloned.1.call-done = f32[128,256]{1,0:T(8,128)} async-done(((f32[128,256]{1,0:T(8,128)}), f32[128,256]{1,0:T(8,128)}) %all-reduce.2.cloned.1.call-update) | async-done | bytes 131088 | tf_op jit(solution)/shard_map/psum | solution.py:77
  239.8 1.6 broadcast_multiply_fusion
  241.4 20.1 %reduce-scatter.5.cloned.1.call-done = f32[128,128]{1,0:T(8,128)} async-done(((f32[512,128]{1,0:T(8,128)}), f32[128,128]{1,0:T(8,128)}) %reduce-scatter.5.cloned.1.call-update) | async-done | bytes 65552 | tf_op jit(solution)/shard_map/reduce_scatter | solution.py:101
  261.5 1.5 convert_element_type.33
  (19 shorter events, 0.1 us)
Async XLA Ops:
  7.2 76.8 %copy-start = (bf16[128,256]{1,0:T(8,128)(2,1)S(1)}, bf16[128,256]{1,0:T(8,128)(2,1)}, u32[]{:S(2)}) copy-start(bf16[128,256]{1,0:T(8,128)(2,1)} %param.9) | copy-start | bytes 196612
  7.2 0.7 copy-start.7
  7.2 76.8 %reduce-scatter.3.cloned.1.call-start = ((), (), s32[]{:S(2)}) async-start(), calls=%async_computation.2 | async-start | bytes 589824 | tf_op jit(solution)/shard_map/reduce_scatter | solution.py:66
  8.6 0.7 copy-start.8
  16.7 0.7 copy-start.5
  19.4 0.8 copy-start.1
  19.4 64.5 %copy-start.4 = (bf16[128,256]{1,0:T(8,128)(2,1)S(1)}, bf16[128,256]{1,0:T(8,128)(2,1)}, u32[]{:S(2)}) copy-start(bf16[128,256]{1,0:T(8,128)(2,1)} %param.15) | copy-start | bytes 196612
  20.2 63.8 %copy-start.6 = (f32[256]{0:T(256)S(1)}, f32[256]{0:T(256)}, u32[]{:S(2)}) copy-start(f32[256]{0:T(256)} %param.10) | copy-start | bytes 3076
  20.2 219.6 %all-reduce.2.cloned.1.call-start = ((), (), s32[]{:S(2)}) async-start(), calls=%async_computation.4 | async-start | bytes 262144 | tf_op jit(solution)/shard_map/psum | solution.py:77
  85.6 31.6 %copy-start.3 = (f32[128,128]{1,0:T(8,128)S(1)}, f32[128,128]{1,0:T(8,128)}, u32[]{:S(2)}) copy-start(f32[128,128]{1,0:T(8,128)} %reduce-scatter.3.cloned.1.call-done) | copy-start | bytes 196612
  118.1 143.4 %reduce-scatter.5.cloned.1.call-start = ((), (), s32[]{:S(2)}) async-start(), calls=%async_computation.3 | async-start | bytes 327680 | tf_op jit(solution)/shard_map/reduce_scatter | solution.py:101
  120.4 0.7 copy-start.2
Sparse Core Ops, SparseCore 0:
  20.3 63.5 reduce-scatter.2
  118.2 121.5 all-reduce.1
  242.4 19.0 reduce-scatter.4
where the time goes:
time: 270 us; the launch traced here: 269 us
  waiting for transfers between devices  164 us (61%)
  blocking collectives  76 us (28%)
  between operations  13.9 us (5%)
  other arithmetic  7.14 us (3%)
  matrix products  4.08 us (2%)
  local copies, waits for them, and re-layouts  4.05 us (2%)
    psum x1, waiting for transfers between devices, body(): lax.psum((jnp.einsum('nf,nh->fh', aggregated, grad_pre, preferred_element...  80.3 us
    reduce_scatter x1, waiting for transfers between devices, body(): lax.psum_scatter(partial_sums.reshape(target_rows, F_IN), 'src', scatter_...  63.7 us
    psum x1, blocking collectives, body(): lax.psum((jnp.einsum('nf,nh->fh', aggregated, grad_pre, preferred_element...  37.8 us
    all_gather x1, blocking collectives, body(): target_grad = lax.all_gather(grad_pre, 'src', axis=0, tiled=True)  31.6 us
    reduce_scatter x1, waiting for transfers between devices, body(): lax.psum_scatter(back_sums.reshape(-1, F_IN), 'dst', scatter_dimension=0,...  20.1 us
    all_gather x1, blocking collectives, body(): source_rows = lax.all_gather(features, 'dst', axis=0, tiled=True)  6.68 us
  transfers between devices with their start and end apart: 3, of which 3 were waited for; matrix products, arithmetic and copies ran while one was open for 2% of the time, Pallas kernels for 0%

commit v1 on v0

v1 whole, which is shorter than its diff:
```python
import functools
import math

import jax
import jax.numpy as jnp
from jax import lax
from jax.experimental import pallas as pl
from jax.experimental.pallas import tpu as pltpu
from jax.sharding import PartitionSpec as P

TILE = 128
F_IN = 128
F_HID = 256
UNITS = 32
NT = (((1,), (1,)), ((), ()))
F32 = jnp.float32
BF16 = jnp.bfloat16


def flip(me, k):
    out = me
    bit = 1
    while bit <= k:
        if k & bit:
            out = out + bit * (1 - 2 * (lax.div(me, bit) % 2))
        bit *= 2
    return out


def each_peer(n, me, body, order=None):
    if n <= 8 and n & (n - 1) == 0:
        for k in order or range(n - 1, 0, -1):
            body(k, flip(me, k))
    else:

        def step(k, carry):
            body(k, lax.rem(me + k, n))
            return carry

        lax.fori_loop(1, n, step, 0)


def rows(i, n=TILE):
    return pl.ds(pl.multiple_of(i * n, n), n)


def kernel(
    n_src, n_dst, slots, edges,
    tid_ref, cnt_ref, x_ref, w_ref, b_ref, pos_ref, ew_ref, go_ref,
    hid_ref, ig_ref, wg_ref, bg_ref,
    xs, rt, ct, adj, adjt, bsend, brecv, gall, fsend, frecv,
    wsend, wrecv, drecv, wfin,
    xss, xrs, bss, brs, gss, grs, fss, frs, wss, wrs, dss, drs, ass, ars,
):
    me_s = lax.axis_index("src")
    me_d = lax.axis_index("dst")
    per = UNITS // n_src
    src_peers = functools.partial(each_peer, n_src, me_s)
    dst_peers = functools.partial(each_peer, n_dst, me_d)

    def to_src(s, src, dst, ss, rs):
        return pltpu.make_async_remote_copy(
            src_ref=src, dst_ref=dst, send_sem=ss, recv_sem=rs,
            device_id=(s, me_d), device_id_type=pl.DeviceIdType.MESH,
        )

    def to_dst(d, src, dst, ss, rs):
        return pltpu.make_async_remote_copy(
            src_ref=src, dst_ref=dst, send_sem=ss, recv_sem=rs,
            device_id=(me_s, d), device_id_type=pl.DeviceIdType.MESH,
        )

    def feat(k, d):
        return to_dst(d, x_ref, xs.at[rows(me_d)], xss.at[k], xrs.at[k])

    def part(k, s):
        return to_src(s, bsend.at[k], brecv.at[k], bss.at[k], brs.at[k])

    def back(k, s):
        return to_src(s, gall.at[rows(me_s)], gall.at[rows(me_s)], gss.at[k], grs.at[k])

    def wred(k, s):
        return to_src(s, wsend.at[s], wrecv.at[me_s], wss.at[k], wrs.at[k])

    def fin(k, d):
        return to_dst(d, fsend.at[k], frecv.at[k], fss.at[k], frs.at[k])

    def wdst(k, d):
        return to_dst(d, drecv.at[me_d], drecv.at[me_d], dss.at[k], drs.at[k])

    def wall(k, s):
        return to_src(s, wfin.at[me_s], wfin.at[me_s], ass.at[k], ars.at[k])

    barrier = pltpu.get_barrier_semaphore()

    def greet_src(k, s):
        pl.semaphore_signal(barrier, inc=1, device_id=(s, me_d), device_id_type=pl.DeviceIdType.MESH)

    def greet_dst(k, d):
        pl.semaphore_signal(barrier, inc=1, device_id=(me_s, d), device_id_type=pl.DeviceIdType.MESH)

    src_peers(greet_src)
    dst_peers(greet_dst)
    pl.semaphore_wait(barrier, n_src + n_dst - 2)

    dst_peers(lambda k, d: feat(k, d).start())
    xs[rows(me_d), :] = x_ref[...]

    group = math.gcd(slots, 8)
    turns = slots // group
    eb = group * edges
    lane = lax.broadcasted_iota(jnp.int32, (1, edges), 1)

    def build(turn):
        tgt, src, wgt = [], [], []
        for j in range(group):
            t = turn * group + j
            tid = tid_ref[0, 0, t]
            cnt = cnt_ref[0, 0, t]
            p = pos_ref[0, 0, pl.ds(t, 1), :]
            live = lane < cnt
            row = lax.shift_right_logical(p, 7) + lax.div(tid, n_dst) * TILE
            tgt.append(jnp.where(live, row, -1))
            src.append((p & 127) + lax.rem(tid, n_dst) * TILE)
            if turns == 1:
                wgt.append(ew_ref[0, 0].astype(F32)[j : j + 1, :])
            else:
                at = pl.ds(pl.multiple_of(turn * group, group), group)
                wgt.append(ew_ref[0, 0, at, :].astype(F32)[j : j + 1, :])
        tgt = jnp.concatenate(tgt, axis=1)
        src = jnp.concatenate(src, axis=1)
        wgt = jnp.concatenate(wgt, axis=1)
        spot = lax.broadcasted_iota(jnp.int32, (TILE, eb), 0)

        def col_hot(c):
            ct[rows(c), :] = jnp.where(spot + c * TILE == src, 1.0, 0.0).astype(BF16)

        def row_hot(r):
            rt[rows(r), :] = jnp.where(spot + r * TILE == tgt, wgt, 0.0).astype(BF16)

        def fill(r):
            v = lax.dot_general(rt[rows(r), :], ct[...], NT, preferred_element_type=F32).astype(BF16)
            adj[rows(r), :] = v if turns == 1 else adj[rows(r), :] + v

        def fill_t(c):
            v = lax.dot_general(ct[rows(c), :], rt[...], NT, preferred_element_type=F32).astype(BF16)
            adjt[rows(c), :] = v if turns == 1 else adjt[rows(c), :] + v

        for n, f in ((n_dst, col_hot), (n_src, row_hot), (n_src, fill), (n_dst, fill_t)):
            if n <= 8:
                for i in range(n):
                    f(i)
            else:
                pl.loop(0, n)(f)

    if turns == 1:
        build(0)
    else:
        adj[...] = jnp.zeros_like(adj)
        adjt[...] = jnp.zeros_like(adjt)
        pl.loop(0, turns)(build)

    dst_peers(lambda k, d: feat(k, d).wait_recv())

    def send_part(k, s):
        bsend[k] = jnp.dot(adj[rows(s), :], xs[...], preferred_element_type=F32).astype(BF16)
        part(k, s).start()

    src_peers(send_part)
    agg = jnp.dot(adj[rows(me_s), :], xs[...], preferred_element_type=F32)
    if n_src <= 8:
        for k in range(n_src - 1, 0, -1):
            part(k, flip(me_s, k)).wait_recv()
            agg = agg + brecv[k].astype(F32)
    else:

        def take(k, a):
            part(k, lax.rem(me_s + k, n_src)).wait_recv()
            return a + brecv[k].astype(F32)

        agg = lax.fori_loop(1, n_src, take, agg)
    agg = agg.astype(BF16)

    preact = jnp.dot(agg, w_ref[...], preferred_element_type=F32) + b_ref[...]
    sig = jax.nn.sigmoid(preact)
    gp = (go_ref[...].astype(F32) * sig * (1.0 + preact * (1.0 - sig))).astype(BF16)
    gall[rows(me_s), :] = lax.dot_general(gp, w_ref[...], NT, preferred_element_type=F32).astype(BF16)
    src_peers(lambda k, s: back(k, s).start())
    hid_ref[...] = (preact * sig).astype(BF16)

    dw = jnp.dot(agg.astype(F32).T.astype(BF16), gp, preferred_element_type=F32)
    bs = jnp.sum(gp.astype(F32), axis=0, keepdims=True)
    sub = lax.broadcasted_iota(jnp.int32, (8, 128), 0)
    bv = jnp.where(sub == 0, bs[:, :128], jnp.where(sub == 1, bs[:, 128:], 0.0))
    for q in range(UNITS):
        i, h = q // 2, q % 2
        wsend[q // per, q % per] = dw[8 * i : 8 * i + 8, 128 * h : 128 * h + 128]
    for s in range(n_src):
        wsend[s, per] = bv
    wrecv[me_s] = wsend[me_s]
    src_peers(lambda k, s: wred(k, s).start())

    src_peers(lambda k, s: back(k, s).wait_recv())

    def send_fin(k, d):
        fsend[k] = jnp.dot(adjt[rows(d), :], gall[...], preferred_element_type=F32).astype(BF16)
        fin(k, d).start()

    dst_peers(send_fin)
    own = jnp.dot(adjt[rows(me_d), :], gall[...], preferred_element_type=F32)

    src_peers(lambda k, s: wred(k, s).wait_recv())
    total = wrecv[0]
    for s in range(1, n_src):
        total = total + wrecv[s]
    drecv[me_d] = total
    dst_peers(lambda k, d: wdst(k, d).start())

    dst_peers(lambda k, d: fin(k, d).wait_recv())
    for k in range(1, n_dst):
        own = own + frecv[k].astype(F32)
    ig_ref[...] = own.astype(BF16)

    dst_peers(lambda k, d: wdst(k, d).wait_recv())
    total = drecv[0]
    for d in range(1, n_dst):
        total = total + drecv[d]
    scale = 1.0 / math.sqrt(TILE * n_src * n_dst)
    total = total * scale
    wfin[me_s] = total[:per]
    src_peers(lambda k, s: wall(k, s).start())
    bg_ref[:, :128] = total[per, 0:1, :]
    bg_ref[:, 128:] = total[per, 1:2, :]
    src_peers(lambda k, s: wall(k, s).wait_recv())
    for q in range(UNITS):
        i, h = q // 2, q % 2
        wg_ref[8 * i : 8 * i + 8, 128 * h : 128 * h + 128] = wfin[q // per, q % per]

    for n, copies in ((0, (feat, fin, wdst)), (1, (part, back, wred, wall))):
        for c in copies:
            (src_peers if n else dst_peers)(lambda k, p, c=c: c(k, p).wait_send())


def body(n_src, n_dst, features, weight, bias, tile_index, edge_count, edge_pos, edge_weight, grad_out):
    slots, edges = edge_pos.shape[2], edge_pos.shape[3]
    own = features.shape[0]
    eb = math.gcd(slots, 8) * edges
    per = UNITS // n_src
    vm = pl.BlockSpec(memory_space=pltpu.VMEM)
    sm = pl.BlockSpec(memory_space=pltpu.SMEM)
    dma = pltpu.SemaphoreType.DMA
    s_sems = [dma((n_src,)), dma((n_src,))]
    d_sems = [dma((n_dst,)), dma((n_dst,))]
    hidden, input_grad, weight_grad, bias_grad = pl.pallas_call(
        functools.partial(kernel, n_src, n_dst, slots, edges),
        out_shape=(
            jax.ShapeDtypeStruct((own, F_HID), BF16),
            jax.ShapeDtypeStruct((own, F_IN), BF16),
            jax.ShapeDtypeStruct((F_IN, F_HID), F32),
            jax.ShapeDtypeStruct((1, F_HID), F32),
        ),
        in_specs=[sm, sm, vm, vm, vm, vm, vm, vm],
        out_specs=(vm, vm, vm, vm),
        scratch_shapes=[
            pltpu.VMEM((n_dst * TILE, F_IN), BF16),
            pltpu.VMEM((n_src * TILE, eb), BF16),
            pltpu.VMEM((n_dst * TILE, eb), BF16),
            pltpu.VMEM((n_src * TILE, n_dst * TILE), BF16),
            pltpu.VMEM((n_dst * TILE, n_src * TILE), BF16),
            pltpu.VMEM((n_src, TILE, F_IN), BF16),
            pltpu.VMEM((n_src, TILE, F_IN), BF16),
            pltpu.VMEM((n_src * TILE, F_IN), BF16),
            pltpu.VMEM((n_dst, TILE, F_IN), BF16),
            pltpu.VMEM((n_dst, TILE, F_IN), BF16),
            pltpu.VMEM((n_src, per + 1, 8, 128), F32),
            pltpu.VMEM((n_src, per + 1, 8, 128), F32),
            pltpu.VMEM((n_dst, per + 1, 8, 128), F32),
            pltpu.VMEM((n_src, per, 8, 128), F32),
            *d_sems, *s_sems, *s_sems, *d_sems, *s_sems, *d_sems, *s_sems,
        ],
        compiler_params=pltpu.CompilerParams(
            collective_id=0, has_side_effects=True,
            vmem_limit_bytes=(24 if slots <= 8 else 60) << 20,
        ),
    )(tile_index, edge_count, features, weight, bias.reshape(1, -1), edge_pos, edge_weight, grad_out)
    return hidden, input_grad, weight_grad, bias_grad.reshape(-1)


def solution(mesh):
    placed = (
        P(("src", "dst"), None),
        P(),
        P(),
        P("src", "dst", None),
        P("src", "dst", None),
        P("src", "dst", None, None),
        P("src", "dst", None, None),
        P(("src", "dst"), None),
    )
    return jax.shard_map(
        functools.partial(body, mesh.shape["src"], mesh.shape["dst"]),
        mesh=mesh,
        in_specs=placed,
        out_specs=(P(("src", "dst"), None), P(("src", "dst"), None), P(), P()),
        check_vma=False,
    )
```

time: 270 us -> 43.5 us (0.16)
  waiting for transfers between devices: 164 us -> 0 us
  blocking collectives: 76 us -> 0 us
  Pallas kernels: 0 us -> 34.9 us
  between operations: 13.9 us -> 0.67 us
  other arithmetic: 7.14 us -> 0 us
  matrix products: 4.08 us -> 0 us
  local copies, waits for them, and re-layouts: 4.05 us -> 7.6 us
    reduce_scatter x2 -> x0, waiting for transfers between devices: 83.8 us -> none  [the longest x1 63.7 us: body(): lax.psum_scatter(partial_sums.reshape(target_rows, F_IN), 'src', scatter_...]
    psum x1 -> x0, waiting for transfers between devices: 80.3 us -> none  [body(): lax.psum((jnp.einsum('nf,nh->fh', aggregated, grad_pre, preferred_element...]
    all_gather x2 -> x0, blocking collectives: 38.2 us -> none  [the longest x1 31.6 us: body(): target_grad = lax.all_gather(grad_pre, 'src', axis=0, tiled=True)]
    psum x1 -> x0, blocking collectives: 37.8 us -> none  [body(): lax.psum((jnp.einsum('nf,nh->fh', aggregated, grad_pre, preferred_element...]
    pallas_call x0 -> x1, Pallas kernels: none -> 34.9 us  [body(): pl.pallas_call(functools.partial(kernel, n_src, n_dst, slots, edges), out...]
    unnamed x18 -> x20, local copies, waits for them, and re-layouts: 2.8 us -> 7.6 us
    dot_general x6 -> x0, matrix products: 4.08 us -> none  [the longest x1 1.68 us: body(): jnp.dot(aggregated, weight, preferred_element_type=jnp.float32) + bias]
  transfers between devices with their start and end apart: 3 -> 0, of which waited for: 3 -> 0; matrix products, arithmetic and copies ran while one was open for 2% -> 0% of each run, Pallas kernels for 0% -> 0%
where the time goes in v1:
time: 43.5 us; the launch traced here: 43.2 us
  Pallas kernels  34.9 us (80%)
  local copies, waits for them, and re-layouts  7.6 us (17%)
  between operations  0.67 us (2%)
    pallas_call x1, Pallas kernels, body(): pl.pallas_call(functools.partial(kernel, n_src, n_dst, slots, edges), out...  34.9 us
    unnamed x20, local copies, waits for them, and re-layouts  7.6 us

profile of v1, /device:TPU:0, one launch (start us, length us, event | category | flops | bytes accessed | tf_op | source)
XLA Modules:
  0.0 43.2 jit_solution(1655215435642957032)
XLA Ops:
  0.6 0.0 copy-start.6
  0.6 0.0 copy-start.5
  0.7 0.6 %copy-done.6 = s32[1,1,8]{2,1,0:T(1,128)S(1)} copy-done((s32[1,1,8]{2,1,0:T(1,128)S(1)}, s32[1,1,8]{2,1,0:T(1,128)}, u32[]{:S(2)}) %copy-start.6) | copy-done | bytes 56
  1.3 0.0 copy-done.5
  1.3 0.0 copy-start
  1.3 0.8 %copy-done = bf16[128,256]{1,0:T(8,128)(2,1)S(1)} copy-done((bf16[128,256]{1,0:T(8,128)(2,1)S(1)}, bf16[128,256]{1,0:T(8,128)(2,1)}, u32[]{:S(2)}) %copy-start) | copy-done | bytes 65560
  2.2 0.0 copy-start.1
  2.2 0.8 %copy-done.1 = bf16[128,256]{1,0:T(8,128)(2,1)S(1)} copy-done((bf16[128,256]{1,0:T(8,128)(2,1)S(1)}, bf16[128,256]{1,0:T(8,128)(2,1)}, u32[]{:S(2)}) %copy-start.1) | copy-done | bytes 65560
  3.0 0.0 copy-start.2
  3.0 0.8 %copy-done.2 = bf16[128,128]{1,0:T(8,128)(2,1)S(1)} copy-done((bf16[128,128]{1,0:T(8,128)(2,1)S(1)}, bf16[128,128]{1,0:T(8,128)(2,1)}, u32[]{:S(2)}) %copy-start.2) | copy-done | bytes 32792
  3.8 0.0 copy-start.3
  3.8 0.7 %copy-done.3 = s32[1,1,8,64]{3,2,1,0:T(8,128)S(1)} copy-done((s32[1,1,8,64]{3,2,1,0:T(8,128)S(1)}, s32[1,1,8,64]{3,2,1,0:T(8,128)}, u32[]{:S(2)}) %copy-start.3) | copy-done | bytes 2072
  4.5 0.0 copy-start.4
  4.5 0.7 %copy-done.4 = bf16[1,1,8,64]{3,2,1,0:T(8,128)(2,1)S(1)} copy-done((bf16[1,1,8,64]{3,2,1,0:T(8,128)(2,1)S(1)}, bf16[1,1,8,64]{3,2,1,0:T(8,128)(2,1)}, u32[]{:S(2)}) %copy-start.4) | copy-done | bytes 1048
  5.1 0.0 copy-start.7
  5.1 0.7 %copy-done.7 = s32[1,1,8]{2,1,0:T(1,128)S(1)} copy-done((s32[1,1,8]{2,1,0:T(1,128)S(1)}, s32[1,1,8]{2,1,0:T(1,128)}, u32[]{:S(2)}) %copy-start.7) | copy-done | bytes 56
  5.8 34.9 %shard_map.111 = (bf16[128,256]{1,0:T(8,128)(2,1)S(1)}, bf16[128,128]{1,0:T(8,128)(2,1)S(1)}, f32[128,256]{1,0:T(8,128)S(1)}, f32[1,256]{1,0:T(1,128)S(1)}) custom-call(s32[1,1,8]{2,1,0:T(1,128)S(1)} %copy-done.6, s32[1,1,8]{2,1,0:T(1,128)S(1)} %copy-done.7, bf16[128,128]{1,0:T(8,128)(2,1)S(1)} %copy-done.2, bf16[128,256]{1,0:T(8,128)(2,1)S(1)} %copy-done, ...), custom_call_target="tpu_custom_call" | custom-call | tf_op jit(solution)/shard_map/pallas_call | solution.py:254
  40.7 0.6 %copy.16 = bf16[128,256]{1,0:T(8,128)(2,1)} copy(bf16[128,256]{1,0:T(8,128)(2,1)S(1)} %get-tuple-element.16) | data formatting | bytes 131072
  41.3 0.6 %copy.17 = bf16[128,128]{1,0:T(8,128)(2,1)} copy(bf16[128,128]{1,0:T(8,128)(2,1)S(1)} %get-tuple-element.17) | data formatting | bytes 65536
  41.9 0.7 %copy.18 = f32[128,256]{1,0:T(8,128)} copy(f32[128,256]{1,0:T(8,128)S(1)} %get-tuple-element.18) | data formatting | bytes 262144
  42.6 0.6 %copy.19 = f32[256]{0:T(256)} copy(f32[256]{0:T(256)S(1)} %bitcast.3) | data formatting | bytes 2048
Async XLA Ops:
  0.6 0.7 %copy-start.6 = (s32[1,1,8]{2,1,0:T(1,128)S(1)}, s32[1,1,8]{2,1,0:T(1,128)}, u32[]{:S(2)}) copy-start(s32[1,1,8]{2,1,0:T(1,128)} %tid_ref.1) | copy-start | bytes 100
  0.6 0.7 %copy-start.5 = (f32[256]{0:T(256)S(1)}, f32[256]{0:T(256)}, u32[]{:S(2)}) copy-start(f32[256]{0:T(256)} %param.10) | copy-start | bytes 3076
  1.3 0.8 %copy-start = (bf16[128,256]{1,0:T(8,128)(2,1)S(1)}, bf16[128,256]{1,0:T(8,128)(2,1)}, u32[]{:S(2)}) copy-start(bf16[128,256]{1,0:T(8,128)(2,1)} %w_ref.1) | copy-start | bytes 196612
  2.2 0.8 %copy-start.1 = (bf16[128,256]{1,0:T(8,128)(2,1)S(1)}, bf16[128,256]{1,0:T(8,128)(2,1)}, u32[]{:S(2)}) copy-start(bf16[128,256]{1,0:T(8,128)(2,1)} %go_ref.1) | copy-start | bytes 196612
  3.0 0.8 %copy-start.2 = (bf16[128,128]{1,0:T(8,128)(2,1)S(1)}, bf16[128,128]{1,0:T(8,128)(2,1)}, u32[]{:S(2)}) copy-start(bf16[128,128]{1,0:T(8,128)(2,1)} %x_ref.1) | copy-start | bytes 98308
  3.8 0.7 %copy-start.3 = (s32[1,1,8,64]{3,2,1,0:T(8,128)S(1)}, s32[1,1,8,64]{3,2,1,0:T(8,128)}, u32[]{:S(2)}) copy-start(s32[1,1,8,64]{3,2,1,0:T(8,128)} %pos_ref.1) | copy-start | bytes 6148
  4.5 0.7 %copy-start.4 = (bf16[1,1,8,64]{3,2,1,0:T(8,128)(2,1)S(1)}, bf16[1,1,8,64]{3,2,1,0:T(8,128)(2,1)}, u32[]{:S(2)}) copy-start(bf16[1,1,8,64]{3,2,1,0:T(8,128)(2,1)} %ew_ref.1) | copy-start | bytes 3076
  5.1 0.7 %copy-start.7 = (s32[1,1,8]{2,1,0:T(1,128)S(1)}, s32[1,1,8]{2,1,0:T(1,128)}, u32[]{:S(2)}) copy-start(s32[1,1,8]{2,1,0:T(1,128)} %cnt_ref.1) | copy-start | bytes 100

commit v2 on v1

--- a/solution.py
+++ b/solution.py
@@ -27,9 +27,9 @@
     return out
 
 
-def each_peer(n, me, body, order=None):
-    if n <= 8 and n & (n - 1) == 0:
-        for k in order or range(n - 1, 0, -1):
+def each_peer(n, me, body):
+    if n <= 8:
+        for k in range(n - 1, 0, -1):
             body(k, flip(me, k))
     else:
 
@@ -46,15 +46,19 @@
 
 def kernel(
     n_src, n_dst, slots, edges,
-    tid_ref, cnt_ref, x_ref, w_ref, b_ref, pos_ref, ew_ref, go_ref,
-    hid_ref, ig_ref, wg_ref, bg_ref,
+    tid_ref, cnt_ref, x_hbm, w_hbm, b_hbm, pos_hbm, ew_hbm, go_hbm,
+    hid_out, ig_out, wg_out, bg_out,
+    hid_ref, ig_ref, wg_ref, bg_ref, outs,
+    x_ref, w_ref, b_ref, pos_ref, ew_ref, go_ref,
     xs, rt, ct, adj, adjt, bsend, brecv, gall, fsend, frecv,
-    wsend, wrecv, drecv, wfin,
-    xss, xrs, bss, brs, gss, grs, fss, frs, wss, wrs, dss, drs, ass, ars,
+    wsend, drecv, ssend, srecv, wcol, wfin,
+    ins, xss, xrs, bss, brs, gss, grs, fss, frs, dss, drs, wss, wrs, css, crs, ass, ars,
 ):
     me_s = lax.axis_index("src")
     me_d = lax.axis_index("dst")
-    per = UNITS // n_src
+    relay = n_src == 8
+    ud = UNITS // n_dst
+    pu = ud // n_src
     src_peers = functools.partial(each_peer, n_src, me_s)
     dst_peers = functools.partial(each_peer, n_dst, me_d)
 
@@ -74,22 +78,46 @@
         return to_dst(d, x_ref, xs.at[rows(me_d)], xss.at[k], xrs.at[k])
 
     def part(k, s):
+        if relay and k in (5, 7):
+            s = flip(me_s, 1)
         return to_src(s, bsend.at[k], brecv.at[k], bss.at[k], brs.at[k])
 
     def back(k, s):
-        return to_src(s, gall.at[rows(me_s)], gall.at[rows(me_s)], gss.at[k], grs.at[k])
-
-    def wred(k, s):
-        return to_src(s, wsend.at[s], wrecv.at[me_s], wss.at[k], wrs.at[k])
+        block = me_s
+        if relay and k in (5, 7):
+            s, block = flip(me_s, 1), flip(me_s, k - 1)
+        return to_src(s, gall.at[rows(block)], gall.at[rows(block)], gss.at[k], grs.at[k])
 
     def fin(k, d):
         return to_dst(d, fsend.at[k], frecv.at[k], fss.at[k], frs.at[k])
 
     def wdst(k, d):
-        return to_dst(d, drecv.at[me_d], drecv.at[me_d], dss.at[k], drs.at[k])
-
-    def wall(k, s):
-        return to_src(s, wfin.at[me_s], wfin.at[me_s], ass.at[k], ars.at[k])
+        return to_dst(d, wsend.at[d], drecv.at[me_d], dss.at[k], drs.at[k])
+
+    def wsrc(k, s):
+        return to_src(s, ssend.at[s if pu else 0], srecv.at[me_s], wss.at[k], wrs.at[k])
+
+    def wcolumn(k, s):
+        return to_src(s, wcol.at[me_s], wcol.at[me_s], css.at[k], crs.at[k])
+
+    def wall(k, d):
+        return to_dst(d, wfin.at[me_d], wfin.at[me_d], ass.at[k], ars.at[k])
+
+    loads = [
+        pltpu.make_async_copy(a, b, ins.at[i])
+        for i, (a, b) in enumerate((
+            (x_hbm, x_ref), (pos_hbm, pos_ref), (ew_hbm, ew_ref),
+            (w_hbm, w_ref), (b_hbm, b_ref), (go_hbm, go_ref),
+        ))
+    ]
+    for c in loads:
+        c.start()
+    stores = [
+        pltpu.make_async_copy(a, b, outs.at[i])
+        for i, (a, b) in enumerate((
+            (hid_ref, hid_out), (ig_ref, ig_out), (wg_ref, wg_out), (bg_ref, bg_out),
+        ))
+    ]
 
     barrier = pltpu.get_barrier_semaphore()
 
@@ -103,10 +131,14 @@
     dst_peers(greet_dst)
     pl.semaphore_wait(barrier, n_src + n_dst - 2)
 
+    loads[0].wait()
     dst_peers(lambda k, d: feat(k, d).start())
     xs[rows(me_d), :] = x_ref[...]
 
-    group = math.gcd(slots, 8)
+    loads[1].wait()
+    loads[2].wait()
+
+    group = math.gcd(slots, 16)
     turns = slots // group
     eb = group * edges
     lane = lax.broadcasted_iota(jnp.int32, (1, edges), 1)
@@ -162,14 +194,28 @@
 
     dst_peers(lambda k, d: feat(k, d).wait_recv())
 
+    def partial_rows(s):
+        return jnp.dot(adj[rows(s), :], xs[...], preferred_element_type=F32)
+
     def send_part(k, s):
-        bsend[k] = jnp.dot(adj[rows(s), :], xs[...], preferred_element_type=F32).astype(BF16)
+        bsend[k] = partial_rows(s).astype(BF16)
         part(k, s).start()
 
-    src_peers(send_part)
-    agg = jnp.dot(adj[rows(me_s), :], xs[...], preferred_element_type=F32)
-    if n_src <= 8:
-        for k in range(n_src - 1, 0, -1):
+    if relay:
+        for k in (7, 5, 3, 2, 1):
+            send_part(k, flip(me_s, k))
+        for k in (6, 4):
+            far = partial_rows(flip(me_s, k))
+            part(k + 1, me_s).wait_recv()
+            bsend[k] = (far + brecv[k + 1].astype(F32)).astype(BF16)
+            part(k, flip(me_s, k)).start()
+    else:
+        src_peers(send_part)
+    agg = partial_rows(me_s)
+    for c in loads[3:]:
+        c.wait()
+    if relay:
+        for k in (1, 2, 3, 6, 4):
             part(k, flip(me_s, k)).wait_recv()
             agg = agg + brecv[k].astype(F32)
     else:
@@ -185,8 +231,13 @@
     sig = jax.nn.sigmoid(preact)
     gp = (go_ref[...].astype(F32) * sig * (1.0 + preact * (1.0 - sig))).astype(BF16)
     gall[rows(me_s), :] = lax.dot_general(gp, w_ref[...], NT, preferred_element_type=F32).astype(BF16)
-    src_peers(lambda k, s: back(k, s).start())
+    if relay:
+        for k in (6, 4, 1, 2, 3):
+            back(k, flip(me_s, k)).start()
+    else:
+        src_peers(lambda k, s: back(k, s).start())
     hid_ref[...] = (preact * sig).astype(BF16)
+    stores[0].start()
 
     dw = jnp.dot(agg.astype(F32).T.astype(BF16), gp, preferred_element_type=F32)
     bs = jnp.sum(gp.astype(F32), axis=0, keepdims=True)
@@ -194,13 +245,46 @@
     bv = jnp.where(sub == 0, bs[:, :128], jnp.where(sub == 1, bs[:, 128:], 0.0))
     for q in range(UNITS):
         i, h = q // 2, q % 2
-        wsend[q // per, q % per] = dw[8 * i : 8 * i + 8, 128 * h : 128 * h + 128]
-    for s in range(n_src):
-        wsend[s, per] = bv
-    wrecv[me_s] = wsend[me_s]
-    src_peers(lambda k, s: wred(k, s).start())
-
-    src_peers(lambda k, s: back(k, s).wait_recv())
+        wsend[q // ud, q % ud] = dw[8 * i : 8 * i + 8, 128 * h : 128 * h + 128]
+    for d in range(n_dst):
+        wsend[d, ud] = bv
+    drecv[me_d] = wsend[me_d]
+    dst_peers(lambda k, d: wdst(k, d).start())
+
+    if relay:
+        for k in (6, 4):
+            back(k, flip(me_s, k)).wait_recv()
+            back(k + 1, me_s).start()
+
+    def ordered(ref, n):
+        total = ref[0]
+        for i in range(1, n):
+            total = total + ref[i]
+        return total
+
+    scale = 1.0 / math.sqrt(TILE * n_src * n_dst)
+    dst_peers(lambda k, d: wdst(k, d).wait_recv())
+    chunk = ordered(drecv, n_dst)
+    if pu:
+        for s in range(n_src):
+            ssend[s, :pu] = chunk[s * pu : s * pu + pu]
+            ssend[s, pu] = chunk[ud]
+        srecv[me_s] = ssend[me_s]
+    else:
+        ssend[0] = chunk
+        srecv[me_s] = chunk
+    src_peers(lambda k, s: wsrc(k, s).start())
+    src_peers(lambda k, s: wsrc(k, s).wait_recv())
+    total = ordered(srecv, n_src) * scale
+    if pu:
+        wcol[me_s] = total[:pu]
+        src_peers(lambda k, s: wcolumn(k, s).start())
+
+    if relay:
+        for k in (1, 2, 3, 7, 5):
+            back(k, flip(me_s, k)).wait_recv()
+    else:
+        src_peers(lambda k, s: back(k, s).wait_recv())
 
     def send_fin(k, d):
         fsend[k] = jnp.dot(adjt[rows(d), :], gall[...], preferred_element_type=F32).astype(BF16)
@@ -209,59 +293,77 @@
     dst_peers(send_fin)
     own = jnp.dot(adjt[rows(me_d), :], gall[...], preferred_element_type=F32)
 
-    src_peers(lambda k, s: wred(k, s).wait_recv())
-    total = wrecv[0]
-    for s in range(1, n_src):
-        total = total + wrecv[s]
-    drecv[me_d] = total
-    dst_peers(lambda k, d: wdst(k, d).start())
-
-    dst_peers(lambda k, d: fin(k, d).wait_recv())
-    for k in range(1, n_dst):
+    if pu:
+        src_peers(lambda k, s: wcolumn(k, s).wait_recv())
+        wfin[me_d] = wcol[...].reshape(ud * 8, 128).astype(BF16)
+    else:
+        wfin[me_d] = total[:ud].reshape(ud * 8, 128).astype(BF16)
+    dst_peers(lambda k, d: wall(k, d).start())
+    last = -1
+    bg_ref[:, :128] = total[last, 0:1, :]
+    bg_ref[:, 128:] = total[last, 1:2, :]
+    stores[3].start()
+
+    for k in range(n_dst - 1, 0, -1):
+        fin(k, me_d).wait_recv()
         own = own + frecv[k].astype(F32)
     ig_ref[...] = own.astype(BF16)
-
-    dst_peers(lambda k, d: wdst(k, d).wait_recv())
-    total = drecv[0]
-    for d in range(1, n_dst):
-        total = total + drecv[d]
-    scale = 1.0 / math.sqrt(TILE * n_src * n_dst)
-    total = total * scale
-    wfin[me_s] = total[:per]
-    src_peers(lambda k, s: wall(k, s).start())
-    bg_ref[:, :128] = total[per, 0:1, :]
-    bg_ref[:, 128:] = total[per, 1:2, :]
-    src_peers(lambda k, s: wall(k, s).wait_recv())
+    stores[1].start()
+
+    dst_peers(lambda k, d: wall(k, d).wait_recv())
     for q in range(UNITS):
         i, h = q // 2, q % 2
-        wg_ref[8 * i : 8 * i + 8, 128 * h : 128 * h + 128] = wfin[q // per, q % per]
-
-    for n, copies in ((0, (feat, fin, wdst)), (1, (part, back, wred, wall))):
-        for c in copies:
-            (src_peers if n else dst_peers)(lambda k, p, c=c: c(k, p).wait_send())
+        at = 8 * (q % ud)
+        wg_ref[8 * i : 8 * i + 8, 128 * h : 128 * h + 128] = wfin[q // ud, at : at + 8, :].astype(F32)
+    stores[2].start()
+
+    src_copies = (part, back, wsrc, wcolumn) if pu else (part, back, wsrc)
+    for c in (feat, fin, wdst, wall):
+        dst_peers(lambda k, p, c=c: c(k, p).wait_send())
+    for c in src_copies:
+        src_peers(lambda k, p, c=c: c(k, p).wait_send())
+    for c in stores:
+        c.wait()
+
+
+def store(h_in, i_in, w_in, b_in, h_out, i_out, w_out, b_out, sems):
+    pairs = ((h_in, h_out), (i_in, i_out), (w_in, w_out), (b_in, b_out))
+    copies = [pltpu.make_async_copy(a, b, sems.at[i]) for i, (a, b) in enumerate(pairs)]
+    for c in copies:
+        c.start()
+    for c in copies:
+        c.wait()
 
 
 def body(n_src, n_dst, features, weight, bias, tile_index, edge_count, edge_pos, edge_weight, grad_out):
     slots, edges = edge_pos.shape[2], edge_pos.shape[3]
     own = features.shape[0]
-    eb = math.gcd(slots, 8) * edges
-    per = UNITS // n_src
-    vm = pl.BlockSpec(memory_space=pltpu.VMEM)
+    eb = math.gcd(slots, 16) * edges
+    ud = UNITS // n_dst
+    pu = ud // n_src
     sm = pl.BlockSpec(memory_space=pltpu.SMEM)
+    hbm = pl.BlockSpec(memory_space=pltpu.HBM)
+    anyw = pl.BlockSpec(memory_space=pl.ANY)
     dma = pltpu.SemaphoreType.DMA
     s_sems = [dma((n_src,)), dma((n_src,))]
     d_sems = [dma((n_dst,)), dma((n_dst,))]
-    hidden, input_grad, weight_grad, bias_grad = pl.pallas_call(
+    outs = (
+        jax.ShapeDtypeStruct((own, F_HID), BF16),
+        jax.ShapeDtypeStruct((own, F_IN), BF16),
+        jax.ShapeDtypeStruct((F_IN, F_HID), F32),
+        jax.ShapeDtypeStruct((1, F_HID), F32),
+    )
+    arrays = (features, weight, bias.reshape(1, -1), edge_pos, edge_weight, grad_out)
+    piece = (pu or ud) + 1
+    results = pl.pallas_call(
         functools.partial(kernel, n_src, n_dst, slots, edges),
-        out_shape=(
-            jax.ShapeDtypeStruct((own, F_HID), BF16),
-            jax.ShapeDtypeStruct((own, F_IN), BF16),
-            jax.ShapeDtypeStruct((F_IN, F_HID), F32),
-            jax.ShapeDtypeStruct((1, F_HID), F32),
-        ),
-        in_specs=[sm, sm, vm, vm, vm, vm, vm, vm],
-        out_specs=(vm, vm, vm, vm),
+        out_shape=outs,
+        in_specs=[sm, sm, *[hbm] * 6],
+        out_specs=(anyw,) * 4,
         scratch_shapes=[
+            *[pltpu.VMEM(a.shape, a.dtype) for a in outs],
+            dma((4,)),
+            *[pltpu.VMEM(a.shape, a.dtype) for a in arrays],
             pltpu.VMEM((n_dst * TILE, F_IN), BF16),
             pltpu.VMEM((n_src * TILE, eb), BF16),
             pltpu.VMEM((n_dst * TILE, eb), BF16),
@@ -272,17 +374,28 @@
             pltpu.VMEM((n_src * TILE, F_IN), BF16),
             pltpu.VMEM((n_dst, TILE, F_IN), BF16),
             pltpu.VMEM((n_dst, TILE, F_IN), BF16),
-            pltpu.VMEM((n_src, per + 1, 8, 128), F32),
-            pltpu.VMEM((n_src, per + 1, 8, 128), F32),
-            pltpu.VMEM((n_dst, per + 1, 8, 128), F32),
-            pltpu.VMEM((n_src, per, 8, 128), F32),
-            *d_sems, *s_sems, *s_sems, *d_sems, *s_sems, *d_sems, *s_sems,
+            pltpu.VMEM((n_dst, ud + 1, 8, 128), F32),
+            pltpu.VMEM((n_dst, ud + 1, 8, 128), F32),
+            pltpu.VMEM((n_src if pu else 1, piece, 8, 128), F32),
+            pltpu.VMEM((n_src, piece, 8, 128), F32),
+            pltpu.VMEM((n_src, max(pu, 1), 8, 128), F32),
+            pltpu.VMEM((n_dst, ud * 8, 128), BF16),
+            dma((len(arrays),)),
+            *d_sems, *s_sems, *s_sems, *d_sems, *d_sems, *s_sems, *s_sems, *d_sems,
         ],
         compiler_params=pltpu.CompilerParams(
             collective_id=0, has_side_effects=True,
-            vmem_limit_bytes=(24 if slots <= 8 else 60) << 20,
+            vmem_limit_bytes=64 << 20,
         ),
-    )(tile_index, edge_count, features, weight, bias.reshape(1, -1), edge_pos, edge_weight, grad_out)
+    )(tile_index, edge_count, *arrays)
+    hidden, input_grad, weight_grad, bias_grad = pl.pallas_call(
+        store,
+        out_shape=outs,
+        in_specs=[anyw] * 4,
+        out_specs=(anyw,) * 4,
+        scratch_shapes=[dma((4,))],
+        compiler_params=pltpu.CompilerParams(vmem_limit_bytes=64 << 20),
+    )(*results)
     return hidden, input_grad, weight_grad, bias_grad.reshape(-1)
 
 

time: 43.5 us -> 44.1 us (1.014)
  Pallas kernels: 34.9 us -> 43.3 us
  local copies, waits for them, and re-layouts: 7.6 us -> 0 us
    pallas_call x0 -> x1, Pallas kernels: none -> 8.12 us  [body(): pl.pallas_call(store, out_shape=outs, in_specs=[anyw] * 4, out_specs=(any...]
    unnamed x20 -> x0, local copies, waits for them, and re-layouts: 7.6 us -> none
where the time goes in v2:
time: 44.1 us; the launch traced here: 43.9 us
  Pallas kernels  43.3 us (98%)
  between operations  0.64 us (1%)
    pallas_call x1, Pallas kernels, body(): pl.pallas_call(functools.partial(kernel, n_src, n_dst, slots, edges), out...  35.2 us
    pallas_call x1, Pallas kernels, body(): pl.pallas_call(store, out_shape=outs, in_specs=[anyw] * 4, out_specs=(any...  8.12 us

profile of v2, /device:TPU:0, one launch (start us, length us, event | category | flops | bytes accessed | tf_op | source)
XLA Modules:
  0.0 43.9 jit_solution(4299235096646620565)
XLA Ops:
  0.6 35.2 %shard_map.111 = (bf16[128,256]{1,0:T(8,128)(2,1)}, bf16[128,128]{1,0:T(8,128)(2,1)}, f32[128,256]{1,0:T(8,128)}, f32[1,256]{1,0:T(1,128)}) custom-call(s32[1,1,8]{2,1,0:T(1,128)} %tid_ref.1, s32[1,1,8]{2,1,0:T(1,128)} %cnt_ref.1, bf16[128,128]{1,0:T(8,128)(2,1)} %x_hbm.1, bf16[128,256]{1,0:T(8,128)(2,1)} %w_hbm.1, f32[1,256]{1,0:T(1,128)} %bitcast.2, ...), custom_call_target="tpu_custom_call" | custom-call | tf_op jit(solution)/shard_map/pallas_call | solution.py:358
  35.8 8.1 %shard_map.112 = (bf16[128,256]{1,0:T(8,128)(2,1)}, bf16[128,128]{1,0:T(8,128)(2,1)}, f32[128,256]{1,0:T(8,128)}, f32[1,256]{1,0:T(1,128)}) custom-call(bf16[128,256]{1,0:T(8,128)(2,1)} %get-tuple-element.12.h_in, bf16[128,128]{1,0:T(8,128)(2,1)} %get-tuple-element.13.i_in, f32[128,256]{1,0:T(8,128)} %get-tuple-element.14.w_in, f32[1,256]{1,0:T(1,128)} %get-tuple-element.15.b_in), custom_call_target="tpu_custom_call" | custom-call | tf_op jit(solution)/shard_map/pallas_call | solution.py:391

commit v3 on v2

--- a/solution.py
+++ b/solution.py
@@ -12,7 +12,6 @@
 F_IN = 128
 F_HID = 256
 UNITS = 32
-NT = (((1,), (1,)), ((), ()))
 F32 = jnp.float32
 BF16 = jnp.bfloat16
 
@@ -47,10 +46,9 @@
 def kernel(
     n_src, n_dst, slots, edges,
     tid_ref, cnt_ref, x_hbm, w_hbm, b_hbm, pos_hbm, ew_hbm, go_hbm,
-    hid_out, ig_out, wg_out, bg_out,
-    hid_ref, ig_ref, wg_ref, bg_ref, outs,
+    hid_ref, ig_ref, wg_ref, bg_ref,
     x_ref, w_ref, b_ref, pos_ref, ew_ref, go_ref,
-    xs, rt, ct, adj, adjt, bsend, brecv, gall, fsend, frecv,
+    xs, rt, ct, hot_s, hot_t, picked, facc, bacc, wt, bsend, brecv, gall, fsend, frecv,
     wsend, drecv, ssend, srecv, wcol, wfin,
     ins, xss, xrs, bss, brs, gss, grs, fss, frs, dss, drs, wss, wrs, css, crs, ass, ars,
 ):
@@ -75,7 +73,7 @@
         )
 
     def feat(k, d):
-        return to_dst(d, x_ref, xs.at[rows(me_d)], xss.at[k], xrs.at[k])
+        return to_dst(d, x_ref, xs.at[me_d], xss.at[k], xrs.at[k])
 
     def part(k, s):
         if relay and k in (5, 7):
@@ -86,7 +84,7 @@
         block = me_s
         if relay and k in (5, 7):
             s, block = flip(me_s, 1), flip(me_s, k - 1)
-        return to_src(s, gall.at[rows(block)], gall.at[rows(block)], gss.at[k], grs.at[k])
+        return to_src(s, gall.at[block], gall.at[block], gss.at[k], grs.at[k])
 
     def fin(k, d):
         return to_dst(d, fsend.at[k], frecv.at[k], fss.at[k], frs.at[k])
@@ -112,12 +110,6 @@
     ]
     for c in loads:
         c.start()
-    stores = [
-        pltpu.make_async_copy(a, b, outs.at[i])
-        for i, (a, b) in enumerate((
-            (hid_ref, hid_out), (ig_ref, ig_out), (wg_ref, wg_out), (bg_ref, bg_out),
-        ))
-    ]
 
     barrier = pltpu.get_barrier_semaphore()
 
@@ -133,7 +125,7 @@
 
     loads[0].wait()
     dst_peers(lambda k, d: feat(k, d).start())
-    xs[rows(me_d), :] = x_ref[...]
+    xs[me_d] = x_ref[...]
 
     loads[1].wait()
     loads[2].wait()
@@ -143,59 +135,82 @@
     eb = group * edges
     lane = lax.broadcasted_iota(jnp.int32, (1, edges), 1)
 
+    def group_slots(turn):
+        if turns == 1:
+            return slice(None)
+        return pl.ds(pl.multiple_of(turn * group, group), group)
+
     def build(turn):
+        at = group_slots(turn)
+        pos = pos_ref[0, 0, at, :]
+        weights = ew_ref[0, 0, at, :].astype(F32)
+        across = lax.broadcasted_iota(jnp.int32, (edges, TILE), 1)
+        turned = pos.T
         tgt, src, wgt = [], [], []
         for j in range(group):
             t = turn * group + j
             tid = tid_ref[0, 0, t]
-            cnt = cnt_ref[0, 0, t]
-            p = pos_ref[0, 0, pl.ds(t, 1), :]
-            live = lane < cnt
-            row = lax.shift_right_logical(p, 7) + lax.div(tid, n_dst) * TILE
-            tgt.append(jnp.where(live, row, -1))
+            p = pos[j : j + 1, :]
+            tgt.append(lax.shift_right_logical(p, 7) + lax.div(tid, n_dst) * TILE)
             src.append((p & 127) + lax.rem(tid, n_dst) * TILE)
-            if turns == 1:
-                wgt.append(ew_ref[0, 0].astype(F32)[j : j + 1, :])
-            else:
-                at = pl.ds(pl.multiple_of(turn * group, group), group)
-                wgt.append(ew_ref[0, 0, at, :].astype(F32)[j : j + 1, :])
+            wgt.append(jnp.where(lane < cnt_ref[0, 0, t], weights[j : j + 1, :], 0.0))
+            c = turned[:, j : j + 1]
+            hot_s[j] = jnp.where((c & 127) == across, 1.0, 0.0).astype(BF16)
+            hot_t[j] = jnp.where(lax.shift_right_logical(c, 7) == across, 1.0, 0.0).astype(BF16)
         tgt = jnp.concatenate(tgt, axis=1)
         src = jnp.concatenate(src, axis=1)
         wgt = jnp.concatenate(wgt, axis=1)
         spot = lax.broadcasted_iota(jnp.int32, (TILE, eb), 0)
 
         def col_hot(c):
-            ct[rows(c), :] = jnp.where(spot + c * TILE == src, 1.0, 0.0).astype(BF16)
+            ct[rows(c), :] = jnp.where(spot == src - c * TILE, wgt, 0.0).astype(BF16)
 
         def row_hot(r):
-            rt[rows(r), :] = jnp.where(spot + r * TILE == tgt, wgt, 0.0).astype(BF16)
-
-        def fill(r):
-            v = lax.dot_general(rt[rows(r), :], ct[...], NT, preferred_element_type=F32).astype(BF16)
-            adj[rows(r), :] = v if turns == 1 else adj[rows(r), :] + v
-
-        def fill_t(c):
-            v = lax.dot_general(ct[rows(c), :], rt[...], NT, preferred_element_type=F32).astype(BF16)
-            adjt[rows(c), :] = v if turns == 1 else adjt[rows(c), :] + v
-
-        for n, f in ((n_dst, col_hot), (n_src, row_hot), (n_src, fill), (n_dst, fill_t)):
+            rt[rows(r), :] = jnp.where(spot == tgt - r * TILE, wgt, 0.0).astype(BF16)
+
+        for n, f in ((n_src, row_hot), (n_dst, col_hot)):
             if n <= 8:
                 for i in range(n):
                     f(i)
             else:
                 pl.loop(0, n)(f)
 
+    def gather(turn, hot, table, tile_of):
+        for j in range(group):
+            i = tile_of(tid_ref[0, 0, turn * group + j])
+            block = table[i]
+            picked[j * edges : (j + 1) * edges, :] = jnp.dot(
+                hot[j], block, preferred_element_type=F32
+            ).astype(BF16)
+
+    def spread(hot, i):
+        return jnp.dot(hot[rows(i), :], picked[...], preferred_element_type=F32)
+
+    def all_turns(hot, table, tile_of, scatter, acc, n):
+        acc[...] = jnp.zeros_like(acc)
+
+        @pl.loop(0, turns)
+        def _(turn):
+            build(turn)
+            gather(turn, hot, table, tile_of)
+
+            @pl.loop(0, n)
+            def _(i):
+                acc[i] += spread(scatter, i)
+
     if turns == 1:
         build(0)
-    else:
-        adj[...] = jnp.zeros_like(adj)
-        adjt[...] = jnp.zeros_like(adjt)
-        pl.loop(0, turns)(build)
-
+    for c in loads[3:]:
+        c.wait()
+    wt[...] = w_ref[...].astype(F32).T.astype(BF16)
     dst_peers(lambda k, d: feat(k, d).wait_recv())
+    if turns == 1:
+        gather(0, hot_s, xs, lambda tid: lax.rem(tid, n_dst))
+    else:
+        all_turns(hot_s, xs, lambda tid: lax.rem(tid, n_dst), rt, facc, n_src)
 
     def partial_rows(s):
-        return jnp.dot(adj[rows(s), :], xs[...], preferred_element_type=F32)
+        return spread(rt, s) if turns == 1 else facc[s]
 
     def send_part(k, s):
         bsend[k] = partial_rows(s).astype(BF16)
@@ -212,8 +227,6 @@
     else:
         src_peers(send_part)
     agg = partial_rows(me_s)
-    for c in loads[3:]:
-        c.wait()
     if relay:
         for k in (1, 2, 3, 6, 4):
             part(k, flip(me_s, k)).wait_recv()
@@ -230,14 +243,13 @@
     preact = jnp.dot(agg, w_ref[...], preferred_element_type=F32) + b_ref[...]
     sig = jax.nn.sigmoid(preact)
     gp = (go_ref[...].astype(F32) * sig * (1.0 + preact * (1.0 - sig))).astype(BF16)
-    gall[rows(me_s), :] = lax.dot_general(gp, w_ref[...], NT, preferred_element_type=F32).astype(BF16)
+    gall[me_s] = jnp.dot(gp, wt[...], preferred_element_type=F32).astype(BF16)
     if relay:
         for k in (6, 4, 1, 2, 3):
             back(k, flip(me_s, k)).start()
     else:
         src_peers(lambda k, s: back(k, s).start())
     hid_ref[...] = (preact * sig).astype(BF16)
-    stores[0].start()
 
     dw = jnp.dot(agg.astype(F32).T.astype(BF16), gp, preferred_element_type=F32)
     bs = jnp.sum(gp.astype(F32), axis=0, keepdims=True)
@@ -286,12 +298,20 @@
     else:
         src_peers(lambda k, s: back(k, s).wait_recv())
 
+    if turns == 1:
+        gather(0, hot_t, gall, lambda tid: lax.div(tid, n_dst))
+    else:
+        all_turns(hot_t, gall, lambda tid: lax.div(tid, n_dst), ct, bacc, n_dst)
+
+    def back_rows(d):
+        return spread(ct, d) if turns == 1 else bacc[d]
+
     def send_fin(k, d):
-        fsend[k] = jnp.dot(adjt[rows(d), :], gall[...], preferred_element_type=F32).astype(BF16)
+        fsend[k] = back_rows(d).astype(BF16)
         fin(k, d).start()
 
     dst_peers(send_fin)
-    own = jnp.dot(adjt[rows(me_d), :], gall[...], preferred_element_type=F32)
+    own = back_rows(me_d)
 
     if pu:
         src_peers(lambda k, s: wcolumn(k, s).wait_recv())
@@ -302,28 +322,23 @@
     last = -1
     bg_ref[:, :128] = total[last, 0:1, :]
     bg_ref[:, 128:] = total[last, 1:2, :]
-    stores[3].start()
 
     for k in range(n_dst - 1, 0, -1):
         fin(k, me_d).wait_recv()
         own = own + frecv[k].astype(F32)
     ig_ref[...] = own.astype(BF16)
-    stores[1].start()
 
     dst_peers(lambda k, d: wall(k, d).wait_recv())
     for q in range(UNITS):
         i, h = q // 2, q % 2
         at = 8 * (q % ud)
         wg_ref[8 * i : 8 * i + 8, 128 * h : 128 * h + 128] = wfin[q // ud, at : at + 8, :].astype(F32)
-    stores[2].start()
 
     src_copies = (part, back, wsrc, wcolumn) if pu else (part, back, wsrc)
     for c in (feat, fin, wdst, wall):
         dst_peers(lambda k, p, c=c: c(k, p).wait_send())
     for c in src_copies:
         src_peers(lambda k, p, c=c: c(k, p).wait_send())
-    for c in stores:
-        c.wait()
 
 
 def store(h_in, i_in, w_in, b_in, h_out, i_out, w_out, b_out, sems):
@@ -338,9 +353,12 @@
 def body(n_src, n_dst, features, weight, bias, tile_index, edge_count, edge_pos, edge_weight, grad_out):
     slots, edges = edge_pos.shape[2], edge_pos.shape[3]
     own = features.shape[0]
-    eb = math.gcd(slots, 16) * edges
+    group = math.gcd(slots, 16)
+    eb = group * edges
+    many = slots > group
     ud = UNITS // n_dst
     pu = ud // n_src
+    vm = pl.BlockSpec(memory_space=pltpu.VMEM)
     sm = pl.BlockSpec(memory_space=pltpu.SMEM)
     hbm = pl.BlockSpec(memory_space=pltpu.HBM)
     anyw = pl.BlockSpec(memory_space=pl.ANY)
@@ -357,21 +375,23 @@
     piece = (pu or ud) + 1
     results = pl.pallas_call(
         functools.partial(kernel, n_src, n_dst, slots, edges),
-        out_shape=outs,
+        out_shape=tuple(pltpu.VMEM(o.shape, o.dtype) for o in outs),
         in_specs=[sm, sm, *[hbm] * 6],
-        out_specs=(anyw,) * 4,
+        out_specs=(vm,) * 4,
         scratch_shapes=[
-            *[pltpu.VMEM(a.shape, a.dtype) for a in outs],
-            dma((4,)),
             *[pltpu.VMEM(a.shape, a.dtype) for a in arrays],
-            pltpu.VMEM((n_dst * TILE, F_IN), BF16),
+            pltpu.VMEM((n_dst, TILE, F_IN), BF16),
             pltpu.VMEM((n_src * TILE, eb), BF16),
             pltpu.VMEM((n_dst * TILE, eb), BF16),
-            pltpu.VMEM((n_src * TILE, n_dst * TILE), BF16),
-            pltpu.VMEM((n_dst * TILE, n_src * TILE), BF16),
+            pltpu.VMEM((group, edges, TILE), BF16),
+            pltpu.VMEM((group, edges, TILE), BF16),
+            pltpu.VMEM((eb, F_IN), BF16),
+            pltpu.VMEM((n_src if many else 1, TILE, F_IN), F32),
+            pltpu.VMEM((n_dst if many else 1, TILE, F_IN), F32),
+            pltpu.VMEM((F_HID, F_IN), BF16),
             pltpu.VMEM((n_src, TILE, F_IN), BF16),
             pltpu.VMEM((n_src, TILE, F_IN), BF16),
-            pltpu.VMEM((n_src * TILE, F_IN), BF16),
+            pltpu.VMEM((n_src, TILE, F_IN), BF16),
             pltpu.VMEM((n_dst, TILE, F_IN), BF16),
             pltpu.VMEM((n_dst, TILE, F_IN), BF16),
             pltpu.VMEM((n_dst, ud + 1, 8, 128), F32),
@@ -385,7 +405,7 @@
         ],
         compiler_params=pltpu.CompilerParams(
             collective_id=0, has_side_effects=True,
-            vmem_limit_bytes=64 << 20,
+            vmem_limit_bytes=(64 << 20) - (1024 << 10),
         ),
     )(tile_index, edge_count, *arrays)
     hidden, input_grad, weight_grad, bias_grad = pl.pallas_call(
@@ -394,7 +414,6 @@
         in_specs=[anyw] * 4,
         out_specs=(anyw,) * 4,
         scratch_shapes=[dma((4,))],
-        compiler_params=pltpu.CompilerParams(vmem_limit_bytes=64 << 20),
     )(*results)
     return hidden, input_grad, weight_grad, bias_grad.reshape(-1)
 

time: 44.1 us -> 45.8 us (1.039)
  local copies, waits for them, and re-layouts: 0 us -> 2.45 us
  Pallas kernels: 43.3 us -> 42.5 us
    unnamed x0 -> x8, local copies, waits for them, and re-layouts: none -> 2.45 us
    pallas_call x1, Pallas kernels: 35.2 us -> 34.4 us  [body(): pl.pallas_call(functools.partial(kernel, n_src, n_dst, slots, edges), out...]
where the time goes in v3:
time: 45.8 us; the launch traced here: 45.6 us
  Pallas kernels  42.5 us (93%)
  local copies, waits for them, and re-layouts  2.45 us (5%)
  between operations  0.65 us (1%)
    pallas_call x1, Pallas kernels, body(): pl.pallas_call(functools.partial(kernel, n_src, n_dst, slots, edges), out...  34.4 us
    pallas_call x1, Pallas kernels, body(): pl.pallas_call(store, out_shape=outs, in_specs=[anyw] * 4, out_specs=(any...  8.11 us
    unnamed x8, local copies, waits for them, and re-layouts  2.45 us

profile of v3, /device:TPU:0, one launch (start us, length us, event | category | flops | bytes accessed | tf_op | source)
XLA Modules:
  0.0 45.6 jit_solution(596385372444087954)
XLA Ops:
  0.6 34.4 %shard_map.111 = (bf16[128,256]{1,0:T(8,128)(2,1)S(1)}, bf16[128,128]{1,0:T(8,128)(2,1)S(1)}, f32[128,256]{1,0:T(8,128)S(1)}, f32[1,256]{1,0:T(1,128)S(1)}) custom-call(s32[1,1,8]{2,1,0:T(1,128)} %tid_ref.1, s32[1,1,8]{2,1,0:T(1,128)} %cnt_ref.1, bf16[128,128]{1,0:T(8,128)(2,1)} %x_hbm.1, bf16[128,256]{1,0:T(8,128)(2,1)} %w_hbm.1, f32[1,256]{1,0:T(1,128)} %bitcast.2, ...), custom_call_target="tpu_custom_call" | custom-call | tf_op jit(solution)/shard_map/pallas_call | solution.py:376
  35.0 0.0 copy-start
  35.0 0.6 %copy-done = f32[128,256]{1,0:T(8,128)} copy-done((f32[128,256]{1,0:T(8,128)}, f32[128,256]{1,0:T(8,128)S(1)}, u32[]{:S(2)}) %copy-start) | copy-done | bytes 131096
  35.7 0.0 copy-start.1
  35.7 0.6 %copy-done.1 = bf16[128,256]{1,0:T(8,128)(2,1)} copy-done((bf16[128,256]{1,0:T(8,128)(2,1)}, bf16[128,256]{1,0:T(8,128)(2,1)S(1)}, u32[]{:S(2)}) %copy-start.1) | copy-done | bytes 65560
  36.3 0.0 copy-start.2
  36.3 0.6 %copy-done.2 = bf16[128,128]{1,0:T(8,128)(2,1)} copy-done((bf16[128,128]{1,0:T(8,128)(2,1)}, bf16[128,128]{1,0:T(8,128)(2,1)S(1)}, u32[]{:S(2)}) %copy-start.2) | copy-done | bytes 32792
  36.9 0.0 copy-start.3
  36.9 0.6 %copy-done.3 = f32[1,256]{1,0:T(1,128)} copy-done((f32[1,256]{1,0:T(1,128)}, f32[1,256]{1,0:T(1,128)S(1)}, u32[]{:S(2)}) %copy-start.3) | copy-done | bytes 1048
  37.5 8.1 %shard_map.112 = (bf16[128,256]{1,0:T(8,128)(2,1)}, bf16[128,128]{1,0:T(8,128)(2,1)}, f32[128,256]{1,0:T(8,128)}, f32[1,256]{1,0:T(1,128)}) custom-call(bf16[128,256]{1,0:T(8,128)(2,1)} %copy-done.1, bf16[128,128]{1,0:T(8,128)(2,1)} %copy-done.2, f32[128,256]{1,0:T(8,128)} %copy-done, f32[1,256]{1,0:T(1,128)} %copy-done.3), custom_call_target="tpu_custom_call" | custom-call | tf_op jit(solution)/shard_map/pallas_call | solution.py:411
Async XLA Ops:
  35.0 0.6 %copy-start = (f32[128,256]{1,0:T(8,128)}, f32[128,256]{1,0:T(8,128)S(1)}, u32[]{:S(2)}) copy-start(f32[128,256]{1,0:T(8,128)S(1)} %get-tuple-element.14.w_in) | copy-start | bytes 393220
  35.7 0.6 %copy-start.1 = (bf16[128,256]{1,0:T(8,128)(2,1)}, bf16[128,256]{1,0:T(8,128)(2,1)S(1)}, u32[]{:S(2)}) copy-start(bf16[128,256]{1,0:T(8,128)(2,1)S(1)} %get-tuple-element.12.h_in) | copy-start | bytes 196612
  36.3 0.6 %copy-start.2 = (bf16[128,128]{1,0:T(8,128)(2,1)}, bf16[128,128]{1,0:T(8,128)(2,1)S(1)}, u32[]{:S(2)}) copy-start(bf16[128,128]{1,0:T(8,128)(2,1)S(1)} %get-tuple-element.13.i_in) | copy-start | bytes 98308
  36.9 0.6 %copy-start.3 = (f32[1,256]{1,0:T(1,128)}, f32[1,256]{1,0:T(1,128)S(1)}, u32[]{:S(2)}) copy-start(f32[1,256]{1,0:T(1,128)S(1)} %get-tuple-element.15.b_in) | copy-start | bytes 3076

commit v4 on v3

--- a/solution.py
+++ b/solution.py
@@ -47,7 +47,7 @@
     n_src, n_dst, slots, edges,
     tid_ref, cnt_ref, x_hbm, w_hbm, b_hbm, pos_hbm, ew_hbm, go_hbm,
     hid_ref, ig_ref, wg_ref, bg_ref,
-    x_ref, w_ref, b_ref, pos_ref, ew_ref, go_ref,
+    w_ref, b_ref, pos_ref, ew_ref, go_ref,
     xs, rt, ct, hot_s, hot_t, picked, facc, bacc, wt, bsend, brecv, gall, fsend, frecv,
     wsend, drecv, ssend, srecv, wcol, wfin,
     ins, xss, xrs, bss, brs, gss, grs, fss, frs, dss, drs, wss, wrs, css, crs, ass, ars,
@@ -73,17 +73,17 @@
         )
 
     def feat(k, d):
-        return to_dst(d, x_ref, xs.at[me_d], xss.at[k], xrs.at[k])
+        return to_dst(d, x_hbm, xs.at[me_d], xss.at[k], xrs.at[k])
 
     def part(k, s):
-        if relay and k in (5, 7):
+        if relay and k == 5:
             s = flip(me_s, 1)
         return to_src(s, bsend.at[k], brecv.at[k], bss.at[k], brs.at[k])
 
     def back(k, s):
         block = me_s
-        if relay and k in (5, 7):
-            s, block = flip(me_s, 1), flip(me_s, k - 1)
+        if relay and k == 5:
+            s, block = flip(me_s, 1), flip(me_s, 4)
         return to_src(s, gall.at[block], gall.at[block], gss.at[k], grs.at[k])
 
     def fin(k, d):
@@ -104,7 +104,7 @@
     loads = [
         pltpu.make_async_copy(a, b, ins.at[i])
         for i, (a, b) in enumerate((
-            (x_hbm, x_ref), (pos_hbm, pos_ref), (ew_hbm, ew_ref),
+            (x_hbm, xs.at[me_d]), (pos_hbm, pos_ref), (ew_hbm, ew_ref),
             (w_hbm, w_ref), (b_hbm, b_ref), (go_hbm, go_ref),
         ))
     ]
@@ -123,9 +123,7 @@
     dst_peers(greet_dst)
     pl.semaphore_wait(barrier, n_src + n_dst - 2)
 
-    loads[0].wait()
     dst_peers(lambda k, d: feat(k, d).start())
-    xs[me_d] = x_ref[...]
 
     loads[1].wait()
     loads[2].wait()
@@ -203,6 +201,7 @@
     for c in loads[3:]:
         c.wait()
     wt[...] = w_ref[...].astype(F32).T.astype(BF16)
+    loads[0].wait()
     dst_peers(lambda k, d: feat(k, d).wait_recv())
     if turns == 1:
         gather(0, hot_s, xs, lambda tid: lax.rem(tid, n_dst))
@@ -217,18 +216,17 @@
         part(k, s).start()
 
     if relay:
-        for k in (7, 5, 3, 2, 1):
+        for k in (5, 7, 6, 3, 2, 1):
             send_part(k, flip(me_s, k))
-        for k in (6, 4):
-            far = partial_rows(flip(me_s, k))
-            part(k + 1, me_s).wait_recv()
-            bsend[k] = (far + brecv[k + 1].astype(F32)).astype(BF16)
-            part(k, flip(me_s, k)).start()
+        far = partial_rows(flip(me_s, 4))
+        part(5, me_s).wait_recv()
+        bsend[4] = (far + brecv[5].astype(F32)).astype(BF16)
+        part(4, flip(me_s, 4)).start()
     else:
         src_peers(send_part)
     agg = partial_rows(me_s)
     if relay:
-        for k in (1, 2, 3, 6, 4):
+        for k in (1, 2, 3, 6, 7, 4):
             part(k, flip(me_s, k)).wait_recv()
             agg = agg + brecv[k].astype(F32)
     else:
@@ -245,7 +243,7 @@
     gp = (go_ref[...].astype(F32) * sig * (1.0 + preact * (1.0 - sig))).astype(BF16)
     gall[me_s] = jnp.dot(gp, wt[...], preferred_element_type=F32).astype(BF16)
     if relay:
-        for k in (6, 4, 1, 2, 3):
+        for k in (4, 7, 6, 3, 2, 1):
             back(k, flip(me_s, k)).start()
     else:
         src_peers(lambda k, s: back(k, s).start())
@@ -255,28 +253,29 @@
     bs = jnp.sum(gp.astype(F32), axis=0, keepdims=True)
     sub = lax.broadcasted_iota(jnp.int32, (8, 128), 0)
     bv = jnp.where(sub == 0, bs[:, :128], jnp.where(sub == 1, bs[:, 128:], 0.0))
+    units = []
     for q in range(UNITS):
         i, h = q // 2, q % 2
-        wsend[q // ud, q % ud] = dw[8 * i : 8 * i + 8, 128 * h : 128 * h + 128]
+        units.append(dw[8 * i : 8 * i + 8, 128 * h : 128 * h + 128])
     for d in range(n_dst):
-        wsend[d, ud] = bv
+        chunk = jnp.concatenate(units[d * ud : d * ud + ud] + [bv, jnp.zeros_like(bv)], axis=0)
+        wsend[d] = chunk.astype(BF16)
     drecv[me_d] = wsend[me_d]
     dst_peers(lambda k, d: wdst(k, d).start())
 
     if relay:
-        for k in (6, 4):
-            back(k, flip(me_s, k)).wait_recv()
-            back(k + 1, me_s).start()
+        back(4, flip(me_s, 4)).wait_recv()
+        back(5, me_s).start()
 
     def ordered(ref, n):
-        total = ref[0]
+        total = ref[0].astype(F32)
         for i in range(1, n):
-            total = total + ref[i]
+            total = total + ref[i].astype(F32)
         return total
 
     scale = 1.0 / math.sqrt(TILE * n_src * n_dst)
     dst_peers(lambda k, d: wdst(k, d).wait_recv())
-    chunk = ordered(drecv, n_dst)
+    chunk = ordered(drecv, n_dst).reshape(ud + 2, 8, 128)[: ud + 1]
     if pu:
         for s in range(n_src):
             ssend[s, :pu] = chunk[s * pu : s * pu + pu]
@@ -286,31 +285,31 @@
         ssend[0] = chunk
         srecv[me_s] = chunk
     src_peers(lambda k, s: wsrc(k, s).start())
+    if relay:
+        for k in (1, 2, 3, 6, 7, 5):
+            back(k, flip(me_s, k)).wait_recv()
+    else:
+        src_peers(lambda k, s: back(k, s).wait_recv())
+
+    if turns == 1:
+        gather(0, hot_t, gall, lambda tid: lax.div(tid, n_dst))
+    else:
+        all_turns(hot_t, gall, lambda tid: lax.div(tid, n_dst), ct, bacc, n_dst)
+
+    def back_rows(d):
+        return spread(ct, d) if turns == 1 else bacc[d]
+
+    def send_fin(k, d):
+        fsend[k] = back_rows(d).astype(BF16)
+        fin(k, d).start()
+
+    dst_peers(send_fin)
+
     src_peers(lambda k, s: wsrc(k, s).wait_recv())
     total = ordered(srecv, n_src) * scale
     if pu:
         wcol[me_s] = total[:pu]
         src_peers(lambda k, s: wcolumn(k, s).start())
-
-    if relay:
-        for k in (1, 2, 3, 7, 5):
-            back(k, flip(me_s, k)).wait_recv()
-    else:
-        src_peers(lambda k, s: back(k, s).wait_recv())
-
-    if turns == 1:
-        gather(0, hot_t, gall, lambda tid: lax.div(tid, n_dst))
-    else:
-        all_turns(hot_t, gall, lambda tid: lax.div(tid, n_dst), ct, bacc, n_dst)
-
-    def back_rows(d):
-        return spread(ct, d) if turns == 1 else bacc[d]
-
-    def send_fin(k, d):
-        fsend[k] = back_rows(d).astype(BF16)
-        fin(k, d).start()
-
-    dst_peers(send_fin)
     own = back_rows(me_d)
 
     if pu:
@@ -379,7 +378,7 @@
         in_specs=[sm, sm, *[hbm] * 6],
         out_specs=(vm,) * 4,
         scratch_shapes=[
-            *[pltpu.VMEM(a.shape, a.dtype) for a in arrays],
+            *[pltpu.VMEM(a.shape, a.dtype) for a in arrays[1:]],
             pltpu.VMEM((n_dst, TILE, F_IN), BF16),
             pltpu.VMEM((n_src * TILE, eb), BF16),
             pltpu.VMEM((n_dst * TILE, eb), BF16),
@@ -394,8 +393,8 @@
             pltpu.VMEM((n_src, TILE, F_IN), BF16),
             pltpu.VMEM((n_dst, TILE, F_IN), BF16),
             pltpu.VMEM((n_dst, TILE, F_IN), BF16),
-            pltpu.VMEM((n_dst, ud + 1, 8, 128), F32),
-            pltpu.VMEM((n_dst, ud + 1, 8, 128), F32),
+            pltpu.VMEM((n_dst, (ud + 2) * 8, 128), BF16),
+            pltpu.VMEM((n_dst, (ud + 2) * 8, 128), BF16),
             pltpu.VMEM((n_src if pu else 1, piece, 8, 128), F32),
             pltpu.VMEM((n_src, piece, 8, 128), F32),
             pltpu.VMEM((n_src, max(pu, 1), 8, 128), F32),
@@ -411,9 +410,10 @@
     hidden, input_grad, weight_grad, bias_grad = pl.pallas_call(
         store,
         out_shape=outs,
-        in_specs=[anyw] * 4,
+        in_specs=[vm] * 4,
         out_specs=(anyw,) * 4,
         scratch_shapes=[dma((4,))],
+        compiler_params=pltpu.CompilerParams(vmem_limit_bytes=4 << 20),
     )(*results)
     return hidden, input_grad, weight_grad, bias_grad.reshape(-1)
 

time: 45.8 us -> 35.5 us (0.78)
  Pallas kernels: 42.5 us -> 34.7 us
  local copies, waits for them, and re-layouts: 2.45 us -> 0 us
    pallas_call x1, Pallas kernels: 8.11 us -> 0.73 us  [body(): pl.pallas_call(store, out_shape=outs, in_specs=[vm] * 4, out_specs=(anyw,...]
    unnamed x8 -> x0, local copies, waits for them, and re-layouts: 2.45 us -> none
where the time goes in v4:
time: 35.5 us; the launch traced here: 35.4 us
  Pallas kernels  34.7 us (98%)
  between operations  0.64 us (2%)
    pallas_call x1, Pallas kernels, body(): pl.pallas_call(functools.partial(kernel, n_src, n_dst, slots, edges), out...  34 us
    pallas_call x1, Pallas kernels, body(): pl.pallas_call(store, out_shape=outs, in_specs=[vm] * 4, out_specs=(anyw,...  0.73 us

profile of v4, /device:TPU:0, one launch (start us, length us, event | category | flops | bytes accessed | tf_op | source)
XLA Modules:
  0.0 35.4 jit_solution(6354402442337653231)
XLA Ops:
  0.6 34.0 %shard_map.111 = (bf16[128,256]{1,0:T(8,128)(2,1)S(1)}, bf16[128,128]{1,0:T(8,128)(2,1)S(1)}, f32[128,256]{1,0:T(8,128)S(1)}, f32[1,256]{1,0:T(1,128)S(1)}) custom-call(s32[1,1,8]{2,1,0:T(1,128)} %tid_ref.1, s32[1,1,8]{2,1,0:T(1,128)} %cnt_ref.1, bf16[128,128]{1,0:T(8,128)(2,1)} %x_hbm.1, bf16[128,256]{1,0:T(8,128)(2,1)} %w_hbm.1, f32[1,256]{1,0:T(1,128)} %bitcast.2, ...), custom_call_target="tpu_custom_call" | custom-call | tf_op jit(solution)/shard_map/pallas_call | solution.py:375
  34.7 0.7 %shard_map.112 = (bf16[128,256]{1,0:T(8,128)(2,1)}, bf16[128,128]{1,0:T(8,128)(2,1)}, f32[128,256]{1,0:T(8,128)}, f32[1,256]{1,0:T(1,128)}) custom-call(bf16[128,256]{1,0:T(8,128)(2,1)S(1)} %get-tuple-element.12.h_in, bf16[128,128]{1,0:T(8,128)(2,1)S(1)} %get-tuple-element.13.i_in, f32[128,256]{1,0:T(8,128)S(1)} %get-tuple-element.14.w_in, ...), custom_call_target="tpu_custom_call" | custom-call | tf_op jit(solution)/shard_map/pallas_call | solution.py:410

commit v5 on v4

--- a/solution.py
+++ b/solution.py
@@ -49,14 +49,13 @@
     hid_ref, ig_ref, wg_ref, bg_ref,
     w_ref, b_ref, pos_ref, ew_ref, go_ref,
     xs, rt, ct, hot_s, hot_t, picked, facc, bacc, wt, bsend, brecv, gall, fsend, frecv,
-    wsend, drecv, ssend, srecv, wcol, wfin,
-    ins, xss, xrs, bss, brs, gss, grs, fss, frs, dss, drs, wss, wrs, css, crs, ass, ars,
+    wsend, wrecv, drecv, wfin,
+    ins, xss, xrs, bss, brs, gss, grs, fss, frs, wss, wrs, dss, drs, ass, ars,
 ):
     me_s = lax.axis_index("src")
     me_d = lax.axis_index("dst")
-    relay = n_src == 8
-    ud = UNITS // n_dst
-    pu = ud // n_src
+    per = UNITS // n_src
+    piece = wsend.shape[1]
     src_peers = functools.partial(each_peer, n_src, me_s)
     dst_peers = functools.partial(each_peer, n_dst, me_d)
 
@@ -76,30 +75,22 @@
         return to_dst(d, x_hbm, xs.at[me_d], xss.at[k], xrs.at[k])
 
     def part(k, s):
-        if relay and k == 5:
-            s = flip(me_s, 1)
         return to_src(s, bsend.at[k], brecv.at[k], bss.at[k], brs.at[k])
 
     def back(k, s):
-        block = me_s
-        if relay and k == 5:
-            s, block = flip(me_s, 1), flip(me_s, 4)
-        return to_src(s, gall.at[block], gall.at[block], gss.at[k], grs.at[k])
+        return to_src(s, gall.at[me_s], gall.at[me_s], gss.at[k], grs.at[k])
 
     def fin(k, d):
         return to_dst(d, fsend.at[k], frecv.at[k], fss.at[k], frs.at[k])
 
+    def wsrc(k, s):
+        return to_src(s, wsend.at[s], wrecv.at[me_s], wss.at[k], wrs.at[k])
+
     def wdst(k, d):
-        return to_dst(d, wsend.at[d], drecv.at[me_d], dss.at[k], drs.at[k])
-
-    def wsrc(k, s):
-        return to_src(s, ssend.at[s if pu else 0], srecv.at[me_s], wss.at[k], wrs.at[k])
-
-    def wcolumn(k, s):
-        return to_src(s, wcol.at[me_s], wcol.at[me_s], css.at[k], crs.at[k])
-
-    def wall(k, d):
-        return to_dst(d, wfin.at[me_d], wfin.at[me_d], ass.at[k], ars.at[k])
+        return to_dst(d, drecv.at[me_d], drecv.at[me_d], dss.at[k], drs.at[k])
+
+    def wall(k, s):
+        return to_src(s, wfin.at[me_s], wfin.at[me_s], ass.at[k], ars.at[k])
 
     loads = [
         pltpu.make_async_copy(a, b, ins.at[i])
@@ -215,18 +206,10 @@
         bsend[k] = partial_rows(s).astype(BF16)
         part(k, s).start()
 
-    if relay:
-        for k in (5, 7, 6, 3, 2, 1):
-            send_part(k, flip(me_s, k))
-        far = partial_rows(flip(me_s, 4))
-        part(5, me_s).wait_recv()
-        bsend[4] = (far + brecv[5].astype(F32)).astype(BF16)
-        part(4, flip(me_s, 4)).start()
-    else:
-        src_peers(send_part)
+    src_peers(send_part)
     agg = partial_rows(me_s)
-    if relay:
-        for k in (1, 2, 3, 6, 7, 4):
+    if n_src <= 8:
+        for k in range(1, n_src):
             part(k, flip(me_s, k)).wait_recv()
             agg = agg + brecv[k].astype(F32)
     else:
@@ -242,11 +225,7 @@
     sig = jax.nn.sigmoid(preact)
     gp = (go_ref[...].astype(F32) * sig * (1.0 + preact * (1.0 - sig))).astype(BF16)
     gall[me_s] = jnp.dot(gp, wt[...], preferred_element_type=F32).astype(BF16)
-    if relay:
-        for k in (4, 7, 6, 3, 2, 1):
-            back(k, flip(me_s, k)).start()
-    else:
-        src_peers(lambda k, s: back(k, s).start())
+    src_peers(lambda k, s: back(k, s).start())
     hid_ref[...] = (preact * sig).astype(BF16)
 
     dw = jnp.dot(agg.astype(F32).T.astype(BF16), gp, preferred_element_type=F32)
@@ -257,15 +236,11 @@
     for q in range(UNITS):
         i, h = q // 2, q % 2
         units.append(dw[8 * i : 8 * i + 8, 128 * h : 128 * h + 128])
-    for d in range(n_dst):
-        chunk = jnp.concatenate(units[d * ud : d * ud + ud] + [bv, jnp.zeros_like(bv)], axis=0)
-        wsend[d] = chunk.astype(BF16)
-    drecv[me_d] = wsend[me_d]
-    dst_peers(lambda k, d: wdst(k, d).start())
-
-    if relay:
-        back(4, flip(me_s, 4)).wait_recv()
-        back(5, me_s).start()
+    fill = [jnp.zeros_like(bv)] * (piece // 8 - per - 1)
+    for s in range(n_src):
+        wsend[s] = jnp.concatenate(units[s * per : s * per + per] + [bv] + fill, axis=0).astype(BF16)
+    wrecv[me_s] = wsend[me_s]
+    src_peers(lambda k, s: wsrc(k, s).start())
 
     def ordered(ref, n):
         total = ref[0].astype(F32)
@@ -274,22 +249,7 @@
         return total
 
     scale = 1.0 / math.sqrt(TILE * n_src * n_dst)
-    dst_peers(lambda k, d: wdst(k, d).wait_recv())
-    chunk = ordered(drecv, n_dst).reshape(ud + 2, 8, 128)[: ud + 1]
-    if pu:
-        for s in range(n_src):
-            ssend[s, :pu] = chunk[s * pu : s * pu + pu]
-            ssend[s, pu] = chunk[ud]
-        srecv[me_s] = ssend[me_s]
-    else:
-        ssend[0] = chunk
-        srecv[me_s] = chunk
-    src_peers(lambda k, s: wsrc(k, s).start())
-    if relay:
-        for k in (1, 2, 3, 6, 7, 5):
-            back(k, flip(me_s, k)).wait_recv()
-    else:
-        src_peers(lambda k, s: back(k, s).wait_recv())
+    src_peers(lambda k, s: back(k, s).wait_recv())
 
     if turns == 1:
         gather(0, hot_t, gall, lambda tid: lax.div(tid, n_dst))
@@ -306,37 +266,30 @@
     dst_peers(send_fin)
 
     src_peers(lambda k, s: wsrc(k, s).wait_recv())
-    total = ordered(srecv, n_src) * scale
-    if pu:
-        wcol[me_s] = total[:pu]
-        src_peers(lambda k, s: wcolumn(k, s).start())
+    drecv[me_d] = ordered(wrecv, n_src).astype(BF16)
+    dst_peers(lambda k, d: wdst(k, d).start())
     own = back_rows(me_d)
-
-    if pu:
-        src_peers(lambda k, s: wcolumn(k, s).wait_recv())
-        wfin[me_d] = wcol[...].reshape(ud * 8, 128).astype(BF16)
-    else:
-        wfin[me_d] = total[:ud].reshape(ud * 8, 128).astype(BF16)
-    dst_peers(lambda k, d: wall(k, d).start())
-    last = -1
-    bg_ref[:, :128] = total[last, 0:1, :]
-    bg_ref[:, 128:] = total[last, 1:2, :]
+    dst_peers(lambda k, d: wdst(k, d).wait_recv())
+    total = ordered(drecv, n_dst) * scale
+    wfin[me_s] = total.astype(BF16)
+    src_peers(lambda k, s: wall(k, s).start())
+    bg_ref[:, :128] = total[per * 8 : per * 8 + 1, :]
+    bg_ref[:, 128:] = total[per * 8 + 1 : per * 8 + 2, :]
 
     for k in range(n_dst - 1, 0, -1):
         fin(k, me_d).wait_recv()
         own = own + frecv[k].astype(F32)
     ig_ref[...] = own.astype(BF16)
 
-    dst_peers(lambda k, d: wall(k, d).wait_recv())
+    src_peers(lambda k, s: wall(k, s).wait_recv())
     for q in range(UNITS):
         i, h = q // 2, q % 2
-        at = 8 * (q % ud)
-        wg_ref[8 * i : 8 * i + 8, 128 * h : 128 * h + 128] = wfin[q // ud, at : at + 8, :].astype(F32)
-
-    src_copies = (part, back, wsrc, wcolumn) if pu else (part, back, wsrc)
-    for c in (feat, fin, wdst, wall):
+        at = 8 * (q % per)
+        wg_ref[8 * i : 8 * i + 8, 128 * h : 128 * h + 128] = wfin[q // per, at : at + 8, :].astype(F32)
+
+    for c in (feat, fin, wdst):
         dst_peers(lambda k, p, c=c: c(k, p).wait_send())
-    for c in src_copies:
+    for c in (part, back, wsrc, wall):
         src_peers(lambda k, p, c=c: c(k, p).wait_send())
 
 
@@ -355,8 +308,8 @@
     group = math.gcd(slots, 16)
     eb = group * edges
     many = slots > group
-    ud = UNITS // n_dst
-    pu = ud // n_src
+    per = UNITS // n_src
+    piece = (per // 2 + 1) * 16
     vm = pl.BlockSpec(memory_space=pltpu.VMEM)
     sm = pl.BlockSpec(memory_space=pltpu.SMEM)
     hbm = pl.BlockSpec(memory_space=pltpu.HBM)
@@ -371,7 +324,6 @@
         jax.ShapeDtypeStruct((1, F_HID), F32),
     )
     arrays = (features, weight, bias.reshape(1, -1), edge_pos, edge_weight, grad_out)
-    piece = (pu or ud) + 1
     results = pl.pallas_call(
         functools.partial(kernel, n_src, n_dst, slots, edges),
         out_shape=tuple(pltpu.VMEM(o.shape, o.dtype) for o in outs),
@@ -393,14 +345,12 @@
             pltpu.VMEM((n_src, TILE, F_IN), BF16),
             pltpu.VMEM((n_dst, TILE, F_IN), BF16),
             pltpu.VMEM((n_dst, TILE, F_IN), BF16),
-            pltpu.VMEM((n_dst, (ud + 2) * 8, 128), BF16),
-            pltpu.VMEM((n_dst, (ud + 2) * 8, 128), BF16),
-            pltpu.VMEM((n_src if pu else 1, piece, 8, 128), F32),
-            pltpu.VMEM((n_src, piece, 8, 128), F32),
-            pltpu.VMEM((n_src, max(pu, 1), 8, 128), F32),
-            pltpu.VMEM((n_dst, ud * 8, 128), BF16),
+            pltpu.VMEM((n_src, piece, 128), BF16),
+            pltpu.VMEM((n_src, piece, 128), BF16),
+            pltpu.VMEM((n_dst, piece, 128), BF16),
+            pltpu.VMEM((n_src, piece, 128), BF16),
             dma((len(arrays),)),
-            *d_sems, *s_sems, *s_sems, *d_sems, *d_sems, *s_sems, *s_sems, *d_sems,
+            *d_sems, *s_sems, *s_sems, *d_sems, *s_sems, *d_sems, *s_sems,
         ],
         compiler_params=pltpu.CompilerParams(
             collective_id=0, has_side_effects=True,

time: 35.5 us -> 35.1 us (0.989)
  Pallas kernels: 34.7 us -> 34.3 us
    pallas_call x1, Pallas kernels: 34 us -> 33.5 us  [body(): pl.pallas_call(functools.partial(kernel, n_src, n_dst, slots, edges), out...]
where the time goes in v5:
time: 35.1 us; the launch traced here: 34.9 us
  Pallas kernels  34.3 us (98%)
  between operations  0.64 us (2%)
    pallas_call x1, Pallas kernels, body(): pl.pallas_call(functools.partial(kernel, n_src, n_dst, slots, edges), out...  33.5 us
    pallas_call x1, Pallas kernels, body(): pl.pallas_call(store, out_shape=outs, in_specs=[vm] * 4, out_specs=(anyw,...  0.73 us

profile of v5, /device:TPU:0, one launch (start us, length us, event | category | flops | bytes accessed | tf_op | source)
XLA Modules:
  0.0 34.9 jit_solution(14551867359386349685)
XLA Ops:
  0.6 33.5 %shard_map.111 = (bf16[128,256]{1,0:T(8,128)(2,1)S(1)}, bf16[128,128]{1,0:T(8,128)(2,1)S(1)}, f32[128,256]{1,0:T(8,128)S(1)}, f32[1,256]{1,0:T(1,128)S(1)}) custom-call(s32[1,1,8]{2,1,0:T(1,128)} %tid_ref.1, s32[1,1,8]{2,1,0:T(1,128)} %cnt_ref.1, bf16[128,128]{1,0:T(8,128)(2,1)} %x_hbm.1, bf16[128,256]{1,0:T(8,128)(2,1)} %w_hbm.1, f32[1,256]{1,0:T(1,128)} %bitcast.2, ...), custom_call_target="tpu_custom_call" | custom-call | tf_op jit(solution)/shard_map/pallas_call | solution.py:327
  34.2 0.7 %shard_map.112 = (bf16[128,256]{1,0:T(8,128)(2,1)}, bf16[128,128]{1,0:T(8,128)(2,1)}, f32[128,256]{1,0:T(8,128)}, f32[1,256]{1,0:T(1,128)}) custom-call(bf16[128,256]{1,0:T(8,128)(2,1)S(1)} %get-tuple-element.12.h_in, bf16[128,128]{1,0:T(8,128)(2,1)S(1)} %get-tuple-element.13.i_in, f32[128,256]{1,0:T(8,128)S(1)} %get-tuple-element.14.w_in, ...), custom_call_target="tpu_custom_call" | custom-call | tf_op jit(solution)/shard_map/pallas_call | solution.py:360

commit v6 on v4

--- a/solution.py
+++ b/solution.py
@@ -54,7 +54,6 @@
 ):
     me_s = lax.axis_index("src")
     me_d = lax.axis_index("dst")
-    relay = n_src == 8
     ud = UNITS // n_dst
     pu = ud // n_src
     src_peers = functools.partial(each_peer, n_src, me_s)
@@ -76,15 +75,10 @@
         return to_dst(d, x_hbm, xs.at[me_d], xss.at[k], xrs.at[k])
 
     def part(k, s):
-        if relay and k == 5:
-            s = flip(me_s, 1)
         return to_src(s, bsend.at[k], brecv.at[k], bss.at[k], brs.at[k])
 
     def back(k, s):
-        block = me_s
-        if relay and k == 5:
-            s, block = flip(me_s, 1), flip(me_s, 4)
-        return to_src(s, gall.at[block], gall.at[block], gss.at[k], grs.at[k])
+        return to_src(s, gall.at[me_s], gall.at[me_s], gss.at[k], grs.at[k])
 
     def fin(k, d):
         return to_dst(d, fsend.at[k], frecv.at[k], fss.at[k], frs.at[k])
@@ -215,18 +209,10 @@
         bsend[k] = partial_rows(s).astype(BF16)
         part(k, s).start()
 
-    if relay:
-        for k in (5, 7, 6, 3, 2, 1):
-            send_part(k, flip(me_s, k))
-        far = partial_rows(flip(me_s, 4))
-        part(5, me_s).wait_recv()
-        bsend[4] = (far + brecv[5].astype(F32)).astype(BF16)
-        part(4, flip(me_s, 4)).start()
-    else:
-        src_peers(send_part)
+    src_peers(send_part)
     agg = partial_rows(me_s)
-    if relay:
-        for k in (1, 2, 3, 6, 7, 4):
+    if n_src <= 8:
+        for k in range(1, n_src):
             part(k, flip(me_s, k)).wait_recv()
             agg = agg + brecv[k].astype(F32)
     else:
@@ -242,11 +228,7 @@
     sig = jax.nn.sigmoid(preact)
     gp = (go_ref[...].astype(F32) * sig * (1.0 + preact * (1.0 - sig))).astype(BF16)
     gall[me_s] = jnp.dot(gp, wt[...], preferred_element_type=F32).astype(BF16)
-    if relay:
-        for k in (4, 7, 6, 3, 2, 1):
-            back(k, flip(me_s, k)).start()
-    else:
-        src_peers(lambda k, s: back(k, s).start())
+    src_peers(lambda k, s: back(k, s).start())
     hid_ref[...] = (preact * sig).astype(BF16)
 
     dw = jnp.dot(agg.astype(F32).T.astype(BF16), gp, preferred_element_type=F32)
@@ -263,10 +245,6 @@
     drecv[me_d] = wsend[me_d]
     dst_peers(lambda k, d: wdst(k, d).start())
 
-    if relay:
-        back(4, flip(me_s, 4)).wait_recv()
-        back(5, me_s).start()
-
     def ordered(ref, n):
         total = ref[0].astype(F32)
         for i in range(1, n):
@@ -285,11 +263,7 @@
         ssend[0] = chunk
         srecv[me_s] = chunk
     src_peers(lambda k, s: wsrc(k, s).start())
-    if relay:
-        for k in (1, 2, 3, 6, 7, 5):
-            back(k, flip(me_s, k)).wait_recv()
-    else:
-        src_peers(lambda k, s: back(k, s).wait_recv())
+    src_peers(lambda k, s: back(k, s).wait_recv())
 
     if turns == 1:
         gather(0, hot_t, gall, lambda tid: lax.div(tid, n_dst))

time: 35.5 us -> 34.8 us (0.980)
  Pallas kernels: 34.7 us -> 34 us
    pallas_call x1, Pallas kernels: 34 us -> 33.2 us  [body(): pl.pallas_call(functools.partial(kernel, n_src, n_dst, slots, edges), out...]
where the time goes in v6:
time: 34.8 us; the launch traced here: 34.6 us
  Pallas kernels  34 us (98%)
  between operations  0.64 us (2%)
    pallas_call x1, Pallas kernels, body(): pl.pallas_call(functools.partial(kernel, n_src, n_dst, slots, edges), out...  33.2 us
    pallas_call x1, Pallas kernels, body(): pl.pallas_call(store, out_shape=outs, in_specs=[vm] * 4, out_specs=(anyw,...  0.73 us

profile of v6, /device:TPU:0, one launch (start us, length us, event | category | flops | bytes accessed | tf_op | source)
XLA Modules:
  0.0 34.6 jit_solution(4040101035861750943)
XLA Ops:
  0.6 33.2 %shard_map.111 = (bf16[128,256]{1,0:T(8,128)(2,1)S(1)}, bf16[128,128]{1,0:T(8,128)(2,1)S(1)}, f32[128,256]{1,0:T(8,128)S(1)}, f32[1,256]{1,0:T(1,128)S(1)}) custom-call(s32[1,1,8]{2,1,0:T(1,128)} %tid_ref.1, s32[1,1,8]{2,1,0:T(1,128)} %cnt_ref.1, bf16[128,128]{1,0:T(8,128)(2,1)} %x_hbm.1, bf16[128,256]{1,0:T(8,128)(2,1)} %w_hbm.1, f32[1,256]{1,0:T(1,128)} %bitcast.2, ...), custom_call_target="tpu_custom_call" | custom-call | tf_op jit(solution)/shard_map/pallas_call | solution.py:349
  33.9 0.7 %shard_map.112 = (bf16[128,256]{1,0:T(8,128)(2,1)}, bf16[128,128]{1,0:T(8,128)(2,1)}, f32[128,256]{1,0:T(8,128)}, f32[1,256]{1,0:T(1,128)}) custom-call(bf16[128,256]{1,0:T(8,128)(2,1)S(1)} %get-tuple-element.12.h_in, bf16[128,128]{1,0:T(8,128)(2,1)S(1)} %get-tuple-element.13.i_in, f32[128,256]{1,0:T(8,128)S(1)} %get-tuple-element.14.w_in, ...), custom_call_target="tpu_custom_call" | custom-call | tf_op jit(solution)/shard_map/pallas_call | solution.py:384

commit v7 on v6

--- a/solution.py
+++ b/solution.py
@@ -12,6 +12,7 @@
 F_IN = 128
 F_HID = 256
 UNITS = 32
+HALF = TILE // 2
 F32 = jnp.float32
 BF16 = jnp.bfloat16
 
@@ -48,7 +49,7 @@
     tid_ref, cnt_ref, x_hbm, w_hbm, b_hbm, pos_hbm, ew_hbm, go_hbm,
     hid_ref, ig_ref, wg_ref, bg_ref,
     w_ref, b_ref, pos_ref, ew_ref, go_ref,
-    xs, rt, ct, hot_s, hot_t, picked, facc, bacc, wt, bsend, brecv, gall, fsend, frecv,
+    xs, rt, ct, hot_s, hot_t, picked, facc, bacc, wt, aggs, gps, bsend, brecv, gall, fsend, frecv,
     wsend, drecv, ssend, srecv, wcol, wfin,
     ins, xss, xrs, bss, brs, gss, grs, fss, frs, dss, drs, wss, wrs, css, crs, ass, ars,
 ):
@@ -74,11 +75,13 @@
     def feat(k, d):
         return to_dst(d, x_hbm, xs.at[me_d], xss.at[k], xrs.at[k])
 
-    def part(k, s):
-        return to_src(s, bsend.at[k], brecv.at[k], bss.at[k], brs.at[k])
-
-    def back(k, s):
-        return to_src(s, gall.at[me_s], gall.at[me_s], gss.at[k], grs.at[k])
+    def part(k, s, h):
+        half = pl.ds(h * HALF, HALF)
+        return to_src(s, bsend.at[k, half], brecv.at[k, half], bss.at[k, h], brs.at[k, h])
+
+    def back(k, s, h):
+        mine = gall.at[me_s, pl.ds(h * HALF, HALF)]
+        return to_src(s, mine, mine, gss.at[k, h], grs.at[k, h])
 
     def fin(k, d):
         return to_dst(d, fsend.at[k], frecv.at[k], fss.at[k], frs.at[k])
@@ -202,35 +205,45 @@
     else:
         all_turns(hot_s, xs, lambda tid: lax.rem(tid, n_dst), rt, facc, n_src)
 
-    def partial_rows(s):
-        return spread(rt, s) if turns == 1 else facc[s]
-
-    def send_part(k, s):
-        bsend[k] = partial_rows(s).astype(BF16)
-        part(k, s).start()
-
-    src_peers(send_part)
-    agg = partial_rows(me_s)
-    if n_src <= 8:
-        for k in range(1, n_src):
-            part(k, flip(me_s, k)).wait_recv()
-            agg = agg + brecv[k].astype(F32)
-    else:
-
-        def take(k, a):
-            part(k, lax.rem(me_s + k, n_src)).wait_recv()
-            return a + brecv[k].astype(F32)
-
-        agg = lax.fori_loop(1, n_src, take, agg)
-    agg = agg.astype(BF16)
-
-    preact = jnp.dot(agg, w_ref[...], preferred_element_type=F32) + b_ref[...]
-    sig = jax.nn.sigmoid(preact)
-    gp = (go_ref[...].astype(F32) * sig * (1.0 + preact * (1.0 - sig))).astype(BF16)
-    gall[me_s] = jnp.dot(gp, wt[...], preferred_element_type=F32).astype(BF16)
-    src_peers(lambda k, s: back(k, s).start())
-    hid_ref[...] = (preact * sig).astype(BF16)
-
+    def partial_rows(s, h):
+        if turns > 1:
+            return facc[s, h * HALF : (h + 1) * HALF, :]
+        at = pl.ds(pl.multiple_of(s * TILE + h * HALF, HALF), HALF)
+        return jnp.dot(rt[at, :], picked[...], preferred_element_type=F32)
+
+    for h in range(2):
+
+        def send_part(k, s, h=h):
+            bsend[k, h * HALF : (h + 1) * HALF, :] = partial_rows(s, h).astype(BF16)
+            part(k, s, h).start()
+
+        src_peers(send_part)
+
+    for h in range(2):
+        half = slice(h * HALF, (h + 1) * HALF)
+        agg = partial_rows(me_s, h)
+        if n_src <= 8:
+            for k in range(1, n_src):
+                part(k, flip(me_s, k), h).wait_recv()
+                agg = agg + brecv[k, half, :].astype(F32)
+        else:
+
+            def take(k, a, h=h, half=half):
+                part(k, lax.rem(me_s + k, n_src), h).wait_recv()
+                return a + brecv[k, half, :].astype(F32)
+
+            agg = lax.fori_loop(1, n_src, take, agg)
+        agg = agg.astype(BF16)
+        aggs[half, :] = agg
+        preact = jnp.dot(agg, w_ref[...], preferred_element_type=F32) + b_ref[...]
+        sig = jax.nn.sigmoid(preact)
+        gp = (go_ref[half, :].astype(F32) * sig * (1.0 + preact * (1.0 - sig))).astype(BF16)
+        gps[half, :] = gp
+        gall[me_s, half, :] = jnp.dot(gp, wt[...], preferred_element_type=F32).astype(BF16)
+        src_peers(lambda k, s, h=h: back(k, s, h).start())
+        hid_ref[half, :] = (preact * sig).astype(BF16)
+
+    agg, gp = aggs[...], gps[...]
     dw = jnp.dot(agg.astype(F32).T.astype(BF16), gp, preferred_element_type=F32)
     bs = jnp.sum(gp.astype(F32), axis=0, keepdims=True)
     sub = lax.broadcasted_iota(jnp.int32, (8, 128), 0)
@@ -263,7 +276,8 @@
         ssend[0] = chunk
         srecv[me_s] = chunk
     src_peers(lambda k, s: wsrc(k, s).start())
-    src_peers(lambda k, s: back(k, s).wait_recv())
+    for h in range(2):
+        src_peers(lambda k, s, h=h: back(k, s, h).wait_recv())
 
     if turns == 1:
         gather(0, hot_t, gall, lambda tid: lax.div(tid, n_dst))
@@ -307,7 +321,10 @@
         at = 8 * (q % ud)
         wg_ref[8 * i : 8 * i + 8, 128 * h : 128 * h + 128] = wfin[q // ud, at : at + 8, :].astype(F32)
 
-    src_copies = (part, back, wsrc, wcolumn) if pu else (part, back, wsrc)
+    for c in (part, back):
+        for h in range(2):
+            src_peers(lambda k, p, c=c, h=h: c(k, p, h).wait_send())
+    src_copies = (wsrc, wcolumn) if pu else (wsrc,)
     for c in (feat, fin, wdst, wall):
         dst_peers(lambda k, p, c=c: c(k, p).wait_send())
     for c in src_copies:
@@ -337,6 +354,7 @@
     anyw = pl.BlockSpec(memory_space=pl.ANY)
     dma = pltpu.SemaphoreType.DMA
     s_sems = [dma((n_src,)), dma((n_src,))]
+    h_sems = [dma((n_src, 2)), dma((n_src, 2))]
     d_sems = [dma((n_dst,)), dma((n_dst,))]
     outs = (
         jax.ShapeDtypeStruct((own, F_HID), BF16),
@@ -362,6 +380,8 @@
             pltpu.VMEM((n_src if many else 1, TILE, F_IN), F32),
             pltpu.VMEM((n_dst if many else 1, TILE, F_IN), F32),
             pltpu.VMEM((F_HID, F_IN), BF16),
+            pltpu.VMEM((TILE, F_IN), BF16),
+            pltpu.VMEM((TILE, F_HID), BF16),
             pltpu.VMEM((n_src, TILE, F_IN), BF16),
             pltpu.VMEM((n_src, TILE, F_IN), BF16),
             pltpu.VMEM((n_src, TILE, F_IN), BF16),
@@ -374,7 +394,7 @@
             pltpu.VMEM((n_src, max(pu, 1), 8, 128), F32),
             pltpu.VMEM((n_dst, ud * 8, 128), BF16),
             dma((len(arrays),)),
-            *d_sems, *s_sems, *s_sems, *d_sems, *d_sems, *s_sems, *s_sems, *d_sems,
+            *d_sems, *h_sems, *h_sems, *d_sems, *d_sems, *s_sems, *s_sems, *d_sems,
         ],
         compiler_params=pltpu.CompilerParams(
             collective_id=0, has_side_effects=True,

time: 34.8 us -> 35.8 us (1.029)
  Pallas kernels: 34 us -> 35 us
    pallas_call x1, Pallas kernels: 33.2 us -> 34.3 us  [body(): pl.pallas_call(functools.partial(kernel, n_src, n_dst, slots, edges), out...]
where the time goes in v7:
time: 35.8 us; the launch traced here: 35.7 us
  Pallas kernels  35 us (98%)
  between operations  0.64 us (2%)
    pallas_call x1, Pallas kernels, body(): pl.pallas_call(functools.partial(kernel, n_src, n_dst, slots, edges), out...  34.3 us
    pallas_call x1, Pallas kernels, body(): pl.pallas_call(store, out_shape=outs, in_specs=[vm] * 4, out_specs=(anyw,...  0.73 us

profile of v7, /device:TPU:0, one launch (start us, length us, event | category | flops | bytes accessed | tf_op | source)
XLA Modules:
  0.0 35.7 jit_solution(18406379171066690100)
XLA Ops:
  0.6 34.3 %shard_map.111 = (bf16[128,256]{1,0:T(8,128)(2,1)S(1)}, bf16[128,128]{1,0:T(8,128)(2,1)S(1)}, f32[128,256]{1,0:T(8,128)S(1)}, f32[1,256]{1,0:T(1,128)S(1)}) custom-call(s32[1,1,8]{2,1,0:T(1,128)} %tid_ref.1, s32[1,1,8]{2,1,0:T(1,128)} %cnt_ref.1, bf16[128,128]{1,0:T(8,128)(2,1)} %x_hbm.1, bf16[128,256]{1,0:T(8,128)(2,1)} %w_hbm.1, f32[1,256]{1,0:T(1,128)} %bitcast.2, ...), custom_call_target="tpu_custom_call" | custom-call | tf_op jit(solution)/shard_map/pallas_call | solution.py:367
  34.9 0.7 %shard_map.112 = (bf16[128,256]{1,0:T(8,128)(2,1)}, bf16[128,128]{1,0:T(8,128)(2,1)}, f32[128,256]{1,0:T(8,128)}, f32[1,256]{1,0:T(1,128)}) custom-call(bf16[128,256]{1,0:T(8,128)(2,1)S(1)} %get-tuple-element.12.h_in, bf16[128,128]{1,0:T(8,128)(2,1)S(1)} %get-tuple-element.13.i_in, f32[128,256]{1,0:T(8,128)S(1)} %get-tuple-element.14.w_in, ...), custom_call_target="tpu_custom_call" | custom-call | tf_op jit(solution)/shard_map/pallas_call | solution.py:404

commit v8 on v6

--- a/solution.py
+++ b/solution.py
@@ -49,13 +49,12 @@
     hid_ref, ig_ref, wg_ref, bg_ref,
     w_ref, b_ref, pos_ref, ew_ref, go_ref,
     xs, rt, ct, hot_s, hot_t, picked, facc, bacc, wt, bsend, brecv, gall, fsend, frecv,
-    wsend, drecv, ssend, srecv, wcol, wfin,
-    ins, xss, xrs, bss, brs, gss, grs, fss, frs, dss, drs, wss, wrs, css, crs, ass, ars,
+    wsend, drecv, srecv, wfin,
+    ins, xss, xrs, bss, brs, gss, grs, fss, frs, dss, drs, wss, wrs, ass, ars,
 ):
     me_s = lax.axis_index("src")
     me_d = lax.axis_index("dst")
     ud = UNITS // n_dst
-    pu = ud // n_src
     src_peers = functools.partial(each_peer, n_src, me_s)
     dst_peers = functools.partial(each_peer, n_dst, me_d)
 
@@ -87,10 +86,7 @@
         return to_dst(d, wsend.at[d], drecv.at[me_d], dss.at[k], drs.at[k])
 
     def wsrc(k, s):
-        return to_src(s, ssend.at[s if pu else 0], srecv.at[me_s], wss.at[k], wrs.at[k])
-
-    def wcolumn(k, s):
-        return to_src(s, wcol.at[me_s], wcol.at[me_s], css.at[k], crs.at[k])
+        return to_src(s, srecv.at[me_s], srecv.at[me_s], wss.at[k], wrs.at[k])
 
     def wall(k, d):
         return to_dst(d, wfin.at[me_d], wfin.at[me_d], ass.at[k], ars.at[k])
@@ -253,15 +249,7 @@
 
     scale = 1.0 / math.sqrt(TILE * n_src * n_dst)
     dst_peers(lambda k, d: wdst(k, d).wait_recv())
-    chunk = ordered(drecv, n_dst).reshape(ud + 2, 8, 128)[: ud + 1]
-    if pu:
-        for s in range(n_src):
-            ssend[s, :pu] = chunk[s * pu : s * pu + pu]
-            ssend[s, pu] = chunk[ud]
-        srecv[me_s] = ssend[me_s]
-    else:
-        ssend[0] = chunk
-        srecv[me_s] = chunk
+    srecv[me_s] = ordered(drecv, n_dst).astype(BF16)
     src_peers(lambda k, s: wsrc(k, s).start())
     src_peers(lambda k, s: back(k, s).wait_recv())
 
@@ -281,20 +269,12 @@
 
     src_peers(lambda k, s: wsrc(k, s).wait_recv())
     total = ordered(srecv, n_src) * scale
-    if pu:
-        wcol[me_s] = total[:pu]
-        src_peers(lambda k, s: wcolumn(k, s).start())
     own = back_rows(me_d)
 
-    if pu:
-        src_peers(lambda k, s: wcolumn(k, s).wait_recv())
-        wfin[me_d] = wcol[...].reshape(ud * 8, 128).astype(BF16)
-    else:
-        wfin[me_d] = total[:ud].reshape(ud * 8, 128).astype(BF16)
+    wfin[me_d] = total[: ud * 8].astype(BF16)
     dst_peers(lambda k, d: wall(k, d).start())
-    last = -1
-    bg_ref[:, :128] = total[last, 0:1, :]
-    bg_ref[:, 128:] = total[last, 1:2, :]
+    bg_ref[:, :128] = total[ud * 8 : ud * 8 + 1, :]
+    bg_ref[:, 128:] = total[ud * 8 + 1 : ud * 8 + 2, :]
 
     for k in range(n_dst - 1, 0, -1):
         fin(k, me_d).wait_recv()
@@ -307,7 +287,7 @@
         at = 8 * (q % ud)
         wg_ref[8 * i : 8 * i + 8, 128 * h : 128 * h + 128] = wfin[q // ud, at : at + 8, :].astype(F32)
 
-    src_copies = (part, back, wsrc, wcolumn) if pu else (part, back, wsrc)
+    src_copies = (part, back, wsrc)
     for c in (feat, fin, wdst, wall):
         dst_peers(lambda k, p, c=c: c(k, p).wait_send())
     for c in src_copies:
@@ -330,7 +310,6 @@
     eb = group * edges
     many = slots > group
     ud = UNITS // n_dst
-    pu = ud // n_src
     vm = pl.BlockSpec(memory_space=pltpu.VMEM)
     sm = pl.BlockSpec(memory_space=pltpu.SMEM)
     hbm = pl.BlockSpec(memory_space=pltpu.HBM)
@@ -345,7 +324,6 @@
         jax.ShapeDtypeStruct((1, F_HID), F32),
     )
     arrays = (features, weight, bias.reshape(1, -1), edge_pos, edge_weight, grad_out)
-    piece = (pu or ud) + 1
     results = pl.pallas_call(
         functools.partial(kernel, n_src, n_dst, slots, edges),
         out_shape=tuple(pltpu.VMEM(o.shape, o.dtype) for o in outs),
@@ -369,12 +347,10 @@
             pltpu.VMEM((n_dst, TILE, F_IN), BF16),
             pltpu.VMEM((n_dst, (ud + 2) * 8, 128), BF16),
             pltpu.VMEM((n_dst, (ud + 2) * 8, 128), BF16),
-            pltpu.VMEM((n_src if pu else 1, piece, 8, 128), F32),
-            pltpu.VMEM((n_src, piece, 8, 128), F32),
-            pltpu.VMEM((n_src, max(pu, 1), 8, 128), F32),
+            pltpu.VMEM((n_src, (ud + 2) * 8, 128), BF16),
             pltpu.VMEM((n_dst, ud * 8, 128), BF16),
             dma((len(arrays),)),
-            *d_sems, *s_sems, *s_sems, *d_sems, *d_sems, *s_sems, *s_sems, *d_sems,
+            *d_sems, *s_sems, *s_sems, *d_sems, *d_sems, *s_sems, *d_sems,
         ],
         compiler_params=pltpu.CompilerParams(
             collective_id=0, has_side_effects=True,

time: 34.8 us -> 32.4 us (0.931)
  Pallas kernels: 34 us -> 31.6 us
    pallas_call x1, Pallas kernels: 33.2 us -> 30.9 us  [body(): pl.pallas_call(functools.partial(kernel, n_src, n_dst, slots, edges), out...]
where the time goes in v8:
time: 32.4 us; the launch traced here: 32.3 us
  Pallas kernels  31.6 us (98%)
  between operations  0.64 us (2%)
    pallas_call x1, Pallas kernels, body(): pl.pallas_call(functools.partial(kernel, n_src, n_dst, slots, edges), out...  30.9 us
    pallas_call x1, Pallas kernels, body(): pl.pallas_call(store, out_shape=outs, in_specs=[vm] * 4, out_specs=(anyw,...  0.73 us

profile of v8, /device:TPU:0, one launch (start us, length us, event | category | flops | bytes accessed | tf_op | source)
XLA Modules:
  0.0 32.3 jit_solution(16997802766298775588)
XLA Ops:
  0.6 30.9 %shard_map.111 = (bf16[128,256]{1,0:T(8,128)(2,1)S(1)}, bf16[128,128]{1,0:T(8,128)(2,1)S(1)}, f32[128,256]{1,0:T(8,128)S(1)}, f32[1,256]{1,0:T(1,128)S(1)}) custom-call(s32[1,1,8]{2,1,0:T(1,128)} %tid_ref.1, s32[1,1,8]{2,1,0:T(1,128)} %cnt_ref.1, bf16[128,128]{1,0:T(8,128)(2,1)} %x_hbm.1, bf16[128,256]{1,0:T(8,128)(2,1)} %w_hbm.1, f32[1,256]{1,0:T(1,128)} %bitcast.2, ...), custom_call_target="tpu_custom_call" | custom-call | tf_op jit(solution)/shard_map/pallas_call | solution.py:327
  31.5 0.7 %shard_map.112 = (bf16[128,256]{1,0:T(8,128)(2,1)}, bf16[128,128]{1,0:T(8,128)(2,1)}, f32[128,256]{1,0:T(8,128)}, f32[1,256]{1,0:T(1,128)}) custom-call(bf16[128,256]{1,0:T(8,128)(2,1)S(1)} %get-tuple-element.12.h_in, bf16[128,128]{1,0:T(8,128)(2,1)S(1)} %get-tuple-element.13.i_in, f32[128,256]{1,0:T(8,128)S(1)} %get-tuple-element.14.w_in, ...), custom_call_target="tpu_custom_call" | custom-call | tf_op jit(solution)/shard_map/pallas_call | solution.py:360
